TPU v7x, 512 devices: a whole 4x8x8 slice. The times are simulated.
512 devices in a mesh: row: 16 (over y, core), col: 32 (over x, z).
Axes of the slice: x: 4, y: 8, z: 8, core: 2. Of those that a mesh axis runs over, the one named last changes fastest.
Arguments:
- covariance: float32 [9216, 9216], P('row', 'col'), may hold values from -1 to 10, as said below
- samples: float32 [192, 9216], P(None, ('col', 'row')), may hold values from -2 to 2
- labels: int32 [192], replicated, may hold values from 0 to 1023
- weights: float32 [9216, 1024], P(('col', 'row')), may hold values from -2.5 to 2.5
Outputs:
- new_covariance: float32 [9216, 9216], P('row', 'col')
- new_weights: float32 [9216, 1024], P(('col', 'row'))
Inputs may be any that keep to these rules, and one draw needn't show every extreme that they name: covariance is symmetric and positive definite.
All inputs are finite; a program needn't handle non-finite values.
Results may differ from a plain program's by a relative error of at most 0.00005.
Values sent between devices are 32-bit elements; how exact they have to be, the bound alone decides.
A program may use at most 64 MiB of HBM per device.

v0:
```python
import jax
import jax.numpy as jnp
from jax import lax
from jax.sharding import Mesh
from jax.sharding import PartitionSpec as P

ROW = ("row_0", "row_1")
COL = ("col_0", "col_1")
COL_ROW = ("col_0", "col_1", "row_0", "row_1")


def from_everyone(value, axis):
    copies = jnp.broadcast_to(value, (lax.axis_size(axis), *value.shape))
    return lax.all_to_all(copies, axis, split_axis=0, concat_axis=0, tiled=True)


def in_order(pieces, dim):
    pieces = jnp.moveaxis(pieces, 0, dim)
    shape = pieces.shape
    return pieces.reshape(*shape[:dim], shape[dim] * shape[dim + 1], *shape[dim + 2 :])


def gathered_copies(value, axis, dim):
    pieces = from_everyone(value, axis)
    return in_order(pieces, dim)


def filled_up(lines, count):
    spare = -len(lines) % count
    return jnp.pad(lines, [(0, spare)] + [(0, 0)] * (lines.ndim - 1))


def split_up(value, dim, count):
    shape = value.shape
    pieces = value.reshape(*shape[:dim], count, shape[dim] // count, *shape[dim + 1 :])
    return jnp.moveaxis(pieces, dim, 0)


def sent_and_summed(value, axis, dim):
    count = lax.axis_size(axis)
    pieces = lax.all_to_all(split_up(value, dim, count), axis, 0, 0, tiled=True)
    return jnp.sum(pieces, axis=0)


def nested_sum(value, axes):
    lines = value.reshape(-1, value.shape[-1])
    padded = filled_up(lines, lax.axis_size(axes))
    whole = gathered_copies(sent_and_summed(padded, axes, 0), axes, 0)
    return lax.slice_in_dim(whole, 0, len(lines)).reshape(value.shape)


def from_root(value, axis, root):
    return lax.dynamic_index_in_dim(lax.all_gather(value, axis), root, 0, keepdims=False)


def sum_in_two_steps(value, axes, dim):
    far, near = axes
    own = sent_and_summed(split_up(value, dim, lax.axis_size(far)), near, dim + 1)
    return jnp.sum(lax.all_to_all(own, far, 0, 0, tiled=True), axis=0)


def whole_of(value, axes, dim):
    far, near = axes
    pieces = from_everyone(from_everyone(value, far), near)
    return in_order(pieces.swapaxes(0, 1).reshape(-1, *value.shape), dim)


def sum_by_parts(value, axes):
    own = sum_in_two_steps(
        filled_up(value, lax.axis_size(axes[0]) * lax.axis_size(axes[1])), axes, 0
    )
    whole = whole_of(own, axes, 0)
    return whole[: len(value)].reshape(value.shape)


def together(arrays, axis):
    line, at, finished = (jnp.concatenate([a.reshape(-1) for a in arrays]), 0, [])
    running = sum_by_parts(line, axis)
    for a in arrays:
        finished.append(running[at : at + a.size].reshape(a.shape))
        at += a.size
    return tuple(finished)


def on_device(covariance, samples, labels, weights):
    precise = lax.Precision.HIGHEST
    row_index = lax.axis_index(ROW)
    col_index = lax.axis_index(COL)
    width_piece = samples.shape[1]
    width_half = covariance.shape[1]
    batch = samples.shape[0]
    x_cols = gathered_copies(samples, ROW, 1)
    classes = lax.broadcasted_iota(jnp.int32, (batch, weights.shape[1]), 1)
    targets = (labels[:, None] == classes).astype(jnp.float32)
    partial_out = jnp.dot(samples, weights, precision=precise, preferred_element_type=jnp.float32)
    row_terms = lax.dot_general(
        x_cols,
        covariance,
        (((1,), (1,)), ((), ())),
        precision=precise,
        preferred_element_type=jnp.float32,
    )
    u_rows = nested_sum(row_terms, COL)
    own_half = lax.dynamic_slice_in_dim(u_rows, col_index % 2 * width_half, width_half, 1)
    u_cols = from_root(own_half, ROW, col_index // 2)
    u_piece = lax.dynamic_slice_in_dim(u_cols, row_index * width_piece, width_piece, 1)
    inner_part = jnp.dot(samples, u_piece.T, precision=precise, preferred_element_type=jnp.float32)
    inner, predicted = together((inner_part, partial_out), (("row_0", "row_1"), ("col_0", "col_1")))
    innovation = 0.5 * (inner + inner.T) + jnp.eye(batch, dtype=jnp.float32)
    factor = jnp.linalg.cholesky(innovation)
    gain_cols = jax.scipy.linalg.cho_solve((factor, True), u_cols)
    new_covariance = covariance - jnp.dot(
        u_rows.T, gain_cols, precision=precise, preferred_element_type=jnp.float32
    )
    gain_piece = lax.dynamic_slice_in_dim(gain_cols, row_index * width_piece, width_piece, 1)
    new_weights = weights + jnp.dot(
        gain_piece.T, targets - predicted, precision=precise, preferred_element_type=jnp.float32
    )
    return (new_covariance, new_weights)


def solution(mesh):
    finer = Mesh(mesh.devices.reshape(8, 2, 4, 8), ("row_0", "row_1", "col_0", "col_1"))
    in_specs = (P(ROW, COL), P(None, COL_ROW), P(), P(COL_ROW, None))
    out_specs = (P(ROW, COL), P(COL_ROW, None))
    return jax.shard_map(
        on_device, mesh=finer, in_specs=in_specs, out_specs=out_specs, check_vma=False
    )
```

profile of v0, /device:TPU:1, one launch (start us, length us, event | category | flops | bytes accessed | tf_op | source)
XLA Modules:
  0.0 303.6 jit_solution(15587678351081563865)
XLA Ops:
  7.2 0.0 copy-start
  7.2 0.8 broadcast_in_dim.15
  8.0 23.9 %all_to_all.43 = f32[16,192,18]{1,2,0:T(8,128)S(1)} all-to-all(f32[16,192,18]{1,2,0:T(8,128)S(1)} %broadcast_in_dim.15), channel_id=1, replica_groups=mesh['row_0'=8,'row_1'=2,'col_0'=4,'col_1'=8] {'row_0','row_1'}, dimensions={0} | all-to-all | bytes 442368 | tf_op jit(solution)/shard_map/all_to_all | solution.py:14
  31.9 0.9 copy.27
  32.8 0.8 dot_general.19
  33.6 0.0 copy-done
  33.6 0.0 copy-start.2
  33.6 0.0 copy-start.3
  33.6 1.1 fusion.1
  34.7 0.3 copy.29
  35.0 31.6 %all_to_all.44 = f32[32,6,576]{2,1,0:T(8,128)S(1)} all-to-all(f32[32,6,576]{2,1,0:T(8,128)S(1)} %copy.29), channel_id=1, replica_groups=mesh['row_0'=8,'row_1'=2,'col_0'=4,'col_1'=8] {'col_0','col_1'}, dimensions={0} | all-to-all | bytes 884736 | tf_op jit(solution)/shard_map/all_to_all | solution.py:41
  66.6 0.1 reduce_sum.27
  66.6 0.9 broadcast_in_dim.16
  67.5 5.8 %all-to-all-start.2 = ((f32[32,6,576]{2,1,0:T(8,128)}), f32[32,6,576]{2,1,0:T(8,128)S(1)}, u32[]{:S(2)}, u32[]{:S(2)}) async-start(f32[32,6,576]{2,1,0:T(8,128)} %broadcast_in_dim.16), calls=%async_computation.2 | async-start | bytes 1310720 | tf_op jit(solution)/shard_map/all_to_all | solution.py:14
  73.3 0.0 all-gather.3.cloned.1.call-start
  73.4 16.8 %all-to-all-done.2 = f32[32,6,576]{2,1,0:T(8,128)S(1)} async-done(((f32[32,6,576]{2,1,0:T(8,128)}), f32[32,6,576]{2,1,0:T(8,128)S(1)}, u32[]{:S(2)}, u32[]{:S(2)}) %all-to-all-start.2) | async-done | bytes 442400 | tf_op jit(solution)/shard_map/all_to_all | solution.py:14
  90.2 0.1 reshape.65
  90.2 0.9 constant_dynamic-slice_fusion
  91.1 0.0 all-gather.3.cloned.1.call-update
  91.2 0.0 copy-done.2
  91.2 0.8 convolution_bitcast_fusion
  92.0 0.1 copy.40
  92.2 39.9 %all-gather.3.cloned.1.call-done = f32[3072,288]{1,0:T(8,128)} async-done(((f32[192,288]{1,0:T(8,128)}), f32[3072,288]{1,0:T(8,128)}) %all-gather.3.cloned.1.call-update) | async-done | bytes 3538960 | tf_op jit(solution)/shard_map/all_gather | solution.py:53
  132.1 1.3 convolution_bitcast_fusion.1
  133.4 0.1 copy.30
  133.5 0.1 reshape.66
  133.6 0.1 pad_maximum_fusion
  133.7 1.0 reshape_reshape.4
  134.7 0.6 copy.31
  135.3 34.9 %all_to_all.45 = f32[32,16,456]{2,1,0:T(8,128)S(1)} all-to-all(f32[32,16,456]{2,1,0:T(8,128)S(1)} %copy.31), channel_id=1, replica_groups=mesh['row_0'=8,'row_1'=2,'col_0'=4,'col_1'=8] {'col_0','col_1'}, dimensions={0} | all-to-all | bytes 1867776 | tf_op jit(solution)/shard_map/all_to_all | solution.py:41
  170.2 0.1 reduce_sum.28
  170.3 15.8 %all_to_all.46 = f32[16,1,456]{2,1,0:T(1,128)S(1)} all-to-all(f32[16,1,456]{2,1,0:T(1,128)S(1)} %all_to_all.31), channel_id=1, replica_groups=mesh['row_0'=8,'row_1'=2,'col_0'=4,'col_1'=8] {'row_0','row_1'}, dimensions={0} | all-to-all | bytes 58368 | tf_op jit(solution)/shard_map/all_to_all | solution.py:59
  186.2 10.3 %all_to_all.47 = f32[16,1,456]{2,1,0:T(1,128)S(1)} all-to-all(f32[16,1,456]{2,1,0:T(1,128)S(1)} %broadcast_in_dim.17), channel_id=1, replica_groups=mesh['row_0'=8,'row_1'=2,'col_0'=4,'col_1'=8] {'row_0','row_1'}, dimensions={0} | all-to-all | bytes 58368 | tf_op jit(solution)/shard_map/all_to_all | solution.py:14
  196.4 1.1 broadcast_in_dim.18
  197.6 5.0 %all-to-all-start.6 = ((f32[32,16,456]{2,1,0:T(8,128)}), f32[32,16,456]{2,1,0:T(8,128)S(1)}, u32[]{:S(2)}, u32[]{:S(2)}) async-start(f32[32,16,456]{2,1,0:T(8,128)} %broadcast_in_dim.18), calls=%async_computation.6 | async-start | bytes 2097152 | tf_op jit(solution)/shard_map/all_to_all | solution.py:14
  202.6 0.6 pad_convert_fusion
  203.3 24.4 %all-to-all-done.6 = f32[32,16,456]{2,1,0:T(8,128)S(1)} async-done(((f32[32,16,456]{2,1,0:T(8,128)}), f32[32,16,456]{2,1,0:T(8,128)S(1)}, u32[]{:S(2)}, u32[]{:S(2)}) %all-to-all-start.6) | async-done | bytes 933920 | tf_op jit(solution)/shard_map/all_to_all | solution.py:14
  227.6 0.6 copy.32
  228.3 1.2 slice.82
  229.5 0.7 slice.103
  230.2 1.7 copy.39
  231.9 1.6 fusion.8
  233.5 1.1 copy.35
  234.6 1.0 fusion.6
  235.5 11.7 %cholesky.51 = f32[128,128]{1,0:T(8,128)S(1)} custom-call(f32[128,128]{1,0:T(8,128)S(1)} %cholesky.124), custom_call_target="Cholesky" | custom-call | tf_op jit(solution)/shard_map/jit(cholesky)/cholesky | solution.py:110
  247.3 9.8 %custom-call.18 = f32[1,128,128]{1,2,0:T(8,128)S(1)} custom-call(f32[1,128,128]{2,1,0:T(8,128)S(1)} %get-tuple-element.23), custom_call_target="InvertDiagBlocksLowerTriangular" | custom-call | tf_op jit(solution)/shard_map/jit(cholesky)/cholesky | solution.py:110
  257.1 0.2 constant_dynamic-update-slice_fusion
  257.3 0.2 convolution_subtract_fusion.3
  257.5 5.8 %cholesky.110 = f32[64,64]{1,0:T(8,128)S(1)} custom-call(f32[64,64]{1,0:T(8,128)S(1)} %convolution_subtract_fusion.3), custom_call_target="Cholesky" | custom-call | tf_op jit(solution)/shard_map/jit(cholesky)/cholesky | solution.py:110
  263.4 0.6 compare_reduce_fusion
  264.0 0.6 compare_reduce_fusion.1
  265.9 0.9 fusion.11
  266.8 19.9 %custom-call.19 = f32[2,128,128]{1,2,0:T(8,128)S(1)} custom-call(f32[2,128,128]{2,1,0:T(8,128)S(1)} %pad_maximum_fusion.3), custom_call_target="InvertDiagBlocksLowerTriangular" | custom-call | tf_op jit(solution)/shard_map/jit(_cho_solve)/triangular_solve | solution.py:111
  286.7 0.0 copy-start.1
  286.7 1.4 fusion.5
  288.2 1.2 convolution_subtract_fusion.2
  289.4 0.3 fusion.17
  289.7 0.2 fusion.16
  289.9 0.4 convolution_subtract_fusion.1
  290.4 0.1 copy.36
  290.5 1.1 slice.84
  291.6 1.1 fusion.14
  292.7 1.8 convolution_subtract_fusion
  294.5 2.2 convolution_add_fusion
  (16 shorter events, 0.2 us)
Async XLA Ops:
  7.2 26.4 %copy-start = (f32[576,288]{0,1:T(8,128)S(1)}, f32[576,288]{0,1:T(8,128)}, u32[]{:S(2)}) copy-start(f32[576,288]{0,1:T(8,128)} %param.4) | copy-start | bytes 1990660
  33.6 57.6 %copy-start.2 = (f32[192,18]{0,1:T(8,128)S(1)}, f32[192,18]{0,1:T(8,128)}, u32[]{:S(2)}) copy-start(f32[192,18]{0,1:T(8,128)} %param.5) | copy-start | bytes 41476
  33.6 57.6 %copy-start.3 = (f32[18,1024]{1,0:T(8,128)S(1)}, f32[18,1024]{1,0:T(8,128)}, u32[]{:S(2)}) copy-start(f32[18,1024]{1,0:T(8,128)} %param.7) | copy-start | bytes 221188
  67.5 22.7 %all-to-all-start.2 = ((f32[32,6,576]{2,1,0:T(8,128)}), f32[32,6,576]{2,1,0:T(8,128)S(1)}, u32[]{:S(2)}, u32[]{:S(2)}) async-start(f32[32,6,576]{2,1,0:T(8,128)} %broadcast_in_dim.16), calls=%async_computation.2 | async-start | bytes 1310720 | tf_op jit(solution)/shard_map/all_to_all | solution.py:14
  73.3 58.8 %all-gather.3.cloned.1.call-start = ((), (), s32[]{:S(2)}) async-start(), calls=%async_computation.7 | async-start | bytes 5013504 | tf_op jit(solution)/shard_map/all_gather | solution.py:53
  197.6 30.0 %all-to-all-start.6 = ((f32[32,16,456]{2,1,0:T(8,128)}), f32[32,16,456]{2,1,0:T(8,128)S(1)}, u32[]{:S(2)}, u32[]{:S(2)}) async-start(f32[32,16,456]{2,1,0:T(8,128)} %broadcast_in_dim.18), calls=%async_computation.6 | async-start | bytes 2097152 | tf_op jit(solution)/shard_map/all_to_all | solution.py:14
  233.5 61.0 %copy-start.4 = (s32[192]{0:T(256)S(1)}, s32[192]{0:T(256)}, u32[]{:S(2)}) copy-start(s32[192]{0:T(256)} %param.6) | copy-start | bytes 2308
  286.7 3.6 %copy-start.1 = (f32[2,128,128]{1,2,0:T(8,128)}, f32[2,128,128]{1,2,0:T(8,128)S(1)}, u32[]{:S(2)}) copy-start(f32[2,128,128]{1,2,0:T(8,128)S(1)} %custom-call.19) | copy-start | bytes 393220
Sparse Core Ops, SparseCore 0:
  91.3 40.7 all-gather.2
where the time goes:
time: 307 us; the launch traced here: 304 us
  blocking collectives  116 us (38%)
  waiting for transfers between devices  81.1 us (26%)
  other arithmetic  53 us (17%)
  between operations  15.6 us (5%)
  local copies, waits for them, and re-layouts  14.4 us (5%)
  matrix products  12.2 us (4%)
  starting transfers between devices  10.8 us (4%)
    all_to_all x2, blocking collectives, sent_and_summed(): pieces = lax.all_to_all(split_up(value, dim, count), axis, 0, 0, tiled=True)  66.4 us
    all_to_all x2, waiting for transfers between devices, from_everyone(): return lax.all_to_all(copies, axis, split_axis=0, concat_axis=0, tiled=True)  41.2 us
    all_gather x1, waiting for transfers between devices, from_root(): lax.all_gather(value, axis)  39.9 us
    all_to_all x2, blocking collectives, from_everyone(): return lax.all_to_all(copies, axis, split_axis=0, concat_axis=0, tiled=True)  34.1 us
    another operation x7, other arithmetic, on_device(): factor = jnp.linalg.cholesky(innovation)  28.7 us
    another operation x6, other arithmetic, on_device(): gain_cols = jax.scipy.linalg.cho_solve((factor, True), u_cols)  21.5 us
    all_to_all x1, blocking collectives, sum_in_two_steps(): return jnp.sum(lax.all_to_all(own, far, 0, 0, tiled=True), axis=0)  15.8 us
    all_to_all x2, starting transfers between devices, from_everyone(): return lax.all_to_all(copies, axis, split_axis=0, concat_axis=0, tiled=True)  10.8 us
  transfers between devices with their start and end apart: 3, of which 3 were waited for; matrix products, arithmetic and copies ran while one was open for 1% of the time, Pallas kernels for 0%

commit v1 on v0

v1 whole, which is shorter than its diff:
```python
import functools

import jax
import jax.numpy as jnp
from jax import lax
from jax.experimental import pallas as pl
from jax.experimental.pallas import tpu as pltpu
from jax.sharding import Mesh
from jax.sharding import PartitionSpec as P

MESH = pl.DeviceIdType.MESH
HIGH = lax.Precision.HIGHEST
F32 = jnp.float32

NY, NK, NX, NZ = 8, 2, 4, 8
B = 192
F = 18
FP = 24
CF, RF = 288, 576
XF = 144
C = 1024
CY = C // NY
SR, DR = 32, 24
AR = SR + DR


def dot(a, b, dims=(((1,), (0,)), ((), ()))):
    return lax.dot_general(a, b, dims, precision=HIGH, preferred_element_type=F32)


TN = (((0,), (0,)), ((), ()))
NT = (((1,), (1,)), ((), ()))


def exchange_kernel(
    cov, xin, win,
    s_out, pr_out, pc_out, pd_out,
    rt, rtp, rp, xpad, wst, xg, x8, x8c, wg, ts, tr, tx, tp, tzr, pz, prc,
    ar, arr, a1, azr, ayr, asum,
    lsem, ssem, s_xy, s_xk, s_x8, s_w, s_t, s_ar, s_tz, s_az, s_ay, s_pz, s_pc, s_pck, s_px, s_s, s_d,
):
    y, k, x, z = (lax.axis_index(a) for a in ("y", "k", "x", "z"))
    col = NZ * x + z
    row = 2 * y + k

    def at(yy=None, kk=None, xx=None, zz=None):
        ids = {}
        for name, v in (("y", yy), ("k", kk), ("x", xx), ("z", zz)):
            if v is not None:
                ids[name] = v
        return ids

    def other(v, d, n):
        return lax.rem(v + d, n)

    sent = []

    def send(src, dst, sem, to, when=None):
        cp = pltpu.make_async_remote_copy(src, dst, ssem, sem, device_id=to, device_id_type=MESH)
        cp.start()
        sent.append(cp)

    fy, fk, fx, fi = col // 4, (col // 2) % 2, 2 * (col % 2) + row // 8, row % 8
    x_is_own = (fy == y) & (fk == k) & (fx == x)
    pcol = 2 * row + x // 2
    gx, gz, gk, gj = pcol // NZ, pcol % NZ, z % 2, 4 * (x % 2) + z // 2
    p_is_own = (gx == x) & (gz == z) & (gk == k)

    barrier = pltpu.get_barrier_semaphore()

    def tell(to):
        pl.semaphore_signal(barrier, inc=1, device_id=to, device_id_type=MESH)

    for d in range(1, NY):
        tell(at(yy=other(y, d, NY)))
    for d in range(1, NZ):
        tell(at(zz=other(z, d, NZ)))
    for d in range(1, 8):
        tell(at(xx=other(x, d // 2, NX), kk=other(k, d % 2, NK)))

    def far_source(i):
        c = 2 * row + x // 2
        return 4 * (x % 2) + i // 2, i % 2, c // NZ, c % NZ

    def far_p_source(j):
        q = 2 * j + k
        return col // 4, (col // 2) % 2, 2 * (col % 2) + q // 8, q % 8

    for i in range(8):
        sy, sk, sx, sz = far_source(i)

        @pl.when(jnp.logical_not((sy == y) & (sk == k) & (sx == x) & (sz == z)))
        def _():
            tell(at(sy, sk, sx, sz))

        py, pk, px, pz_ = far_p_source(i)

        @pl.when(jnp.logical_not((py == y) & (pk == k) & (px == x) & (pz_ == z)))
        def _():
            tell(at(py, pk, px, pz_))

    load = pltpu.make_async_copy(cov, rt, lsem)
    load.start()
    xpad[...] = jnp.zeros_like(xpad)
    xpad[0:F, :] = xin[...]
    xg[k, y] = xpad[...]
    wst[...] = jnp.zeros_like(wst)
    for j in range(NY):
        wst[j, 0:F, :] = win[:, CY * j : CY * (j + 1)]
    wg[y] = wst[y]
    load.wait()
    rtp[...] = jnp.zeros_like(rtp)
    for q in range(16):
        r = 2 * (q % 8) + q // 8
        rtp[FP * q : FP * q + F, :] = rt[F * r : F * r + F, :]
    rp[...] = rtp[...].T

    own = x_is_own.astype(jnp.int32) + p_is_own.astype(jnp.int32)
    pl.semaphore_wait(barrier, 7 + 7 + 7 + 16 - own)

    for d in range(1, NY):
        send(xpad, xg.at[k, y], s_xy.at[d], at(yy=other(y, d, NY)))
    far = []
    for d in range(NZ):
        tz = other(z, d, NZ)
        if d == 0:

            @pl.when(x_is_own)
            def _():
                pltpu.make_async_copy(xpad, x8.at[fi], s_x8.at[fi]).start()

            @pl.when(jnp.logical_not(x_is_own))
            def _():
                pltpu.make_async_remote_copy(
                    xpad, x8.at[fi], ssem, s_x8.at[fi], device_id=at(fy, fk, fx, tz), device_id_type=MESH
                ).start()
        else:
            send(xpad, x8.at[fi], s_x8.at[fi], at(fy, fk, fx, tz))
    for d in range(1, NY):
        ty = other(y, d, NY)
        send(wst.at[ty], wg.at[y], s_w.at[d], at(yy=ty))

    def got(dst, sem):
        pltpu.make_async_copy(dst, dst, sem).wait()

    for d in range(1, NY):
        got(xpad, s_xy.at[d])
    send(xg.at[k], xg.at[k], s_xk, at(kk=1 - k))
    for d in range(1, NY):
        got(wg.at[0], s_w.at[d])
    part = dot(xg[k].reshape(NY * FP, B), wg[...].reshape(NY * FP, CY), TN)
    for q in range(8):
        ar[q, SR:AR, :] = part[DR * q : DR * (q + 1), :]
    got(xg.at[0], s_xk)

    xct = xg[...].reshape(2 * NY * FP, B)
    for d in (2, 1, 3, 0):
        tx_ = other(x, d, NX)
        ts[d] = dot(rp[pl.ds(pl.multiple_of(XF * tx_, 16), XF), :], xct)
        if d:
            send(ts.at[d], tr.at[d], s_t.at[d], at(xx=tx_))
    for i in range(8):
        got(xpad, s_x8.at[i])
    for i in range(8):
        x8c[F * i : F * (i + 1), :] = x8[i, 0:F, :]
    for d in range(1, NX):
        got(tr.at[d], s_t.at[d])
    tx[...] = ts[0] + tr[1] + tr[2] + tr[3]
    inner = dot(x8c[...], tx[...], TN)
    for q in range(4):
        ar[q, 0:SR, :] = inner[SR * q : SR * (q + 1), 0:128]
    for q in range(2):
        ar[4 + q, 0:SR, :] = inner[128 + SR * q : 128 + SR * (q + 1), 0:128]
        ar[6 + q, 0:SR, :] = jnp.zeros((SR, 128), F32)
        ar[6 + q, 0:SR, 0:64] = inner[128 + SR * q : 128 + SR * (q + 1), 128:192]
    for d in range(1, 8):
        tx_, tk_ = other(x, d // 2, NX), other(k, d % 2, NK)
        send(ar.at[2 * tx_ + tk_], arr.at[d], s_ar.at[d], at(xx=tx_, kk=tk_))
    tp[...] = jnp.zeros_like(tp)
    for i in range(8):
        tp[i, 0:F, :] = tx[F * i : F * (i + 1), :]
    for d in range(1, NZ):
        tz = other(z, d, NZ)
        send(tp.at[tz], tzr.at[d], s_tz.at[d], at(zz=tz))

    for d in range(1, 8):
        got(arr.at[d], s_ar.at[d])
    q_own = 2 * x + k
    total = ar[q_own]
    for d in range(1, 8):
        total = total + arr[d]
    a1[...] = total
    for d in range(1, NZ):
        send(a1, azr.at[d], s_az.at[d], at(zz=other(z, d, NZ)))

    for d in range(1, NZ):
        got(tzr.at[d], s_tz.at[d])
    piece = tp[z]
    for d in range(1, NZ):
        piece = piece + tzr[d]
    pz[z] = piece
    for d in range(1, NZ):
        send(pz.at[z], pz.at[z], s_pz.at[d], at(zz=other(z, d, NZ)))
    for d in range(NY):
        ty = other(y, d, NY)
        if d == 0:

            @pl.when(p_is_own)
            def _():
                pltpu.make_async_copy(pz.at[z], pc_out.at[gk, gj], s_pc.at[gj]).start()

            @pl.when(jnp.logical_not(p_is_own))
            def _():
                pltpu.make_async_remote_copy(
                    pz.at[z], pc_out.at[gk, gj], ssem, s_pc.at[gj], device_id=at(ty, gk, gx, gz), device_id_type=MESH
                ).start()
        else:
            send(pz.at[z], pc_out.at[gk, gj], s_pc.at[gj], at(ty, gk, gx, gz))

    for d in range(1, NZ):
        got(azr.at[d], s_az.at[d])
    total = a1[...]
    for d in range(1, NZ):
        total = total + azr[d]
    ayr[y] = total
    for d in range(1, NY):
        send(ayr.at[y], ayr.at[y], s_ay.at[d], at(yy=other(y, d, NY)))

    for d in range(1, NZ):
        got(pz.at[0], s_pz.at[d])
    for i in range(8):
        prc[F * i : F * (i + 1), :] = pz[i, 0:F, :]
    pr_out[x] = prc[...]
    for d in range(1, NX):
        send(prc, pr_out.at[x], s_px.at[d], at(xx=other(x, d, NX)))

    for d in range(1, NY):
        got(ayr.at[0], s_ay.at[d])
    total = ayr[0, 0:SR, :]
    for j in range(1, NY):
        total = total + ayr[j, 0:SR, :]
    asum[...] = total
    s_out[q_own] = total
    pd_out[q_own] = ayr[:, SR:AR, :]
    for d in range(1, 8):
        send(asum, s_out.at[q_own], s_s.at[d], at(xx=other(x, d // 2, NX), kk=other(k, d % 2, NK)))
    for d in range(1, 8):
        send(
            ayr.at[:, pl.ds(SR, DR), :], pd_out.at[q_own], s_d.at[d], at(xx=other(x, d // 2, NX), kk=other(k, d % 2, NK))
        )

    for i in range(8):
        got(xpad, s_pc.at[i])
    send(pc_out.at[k], pc_out.at[k], s_pck, at(kk=1 - k))
    for d in range(1, 8):
        got(asum, s_s.at[d])
    for d in range(1, NX):
        got(prc, s_px.at[d])
    for d in range(1, 8):
        got(pd_out.at[0], s_d.at[d])
    got(pc_out.at[0], s_pck)
    for cp in sent:
        cp.wait_send()

    @pl.when(jnp.logical_not(x_is_own))
    def _():
        got(xpad, ssem)

    @pl.when(jnp.logical_not(p_is_own))
    def _():
        got(xpad, ssem)


def wide(v, n):
    return jnp.broadcast_to(v, (8, n))


def inverse_of_2(a, b, d):
    s = 1.0 / (a * d - b * b)
    return ((d * s, -(b * s)), (-(b * s), a * s))


def inverse_of_4(d):
    two = range(2)
    p = inverse_of_2(d[0][0], d[0][1], d[1][1])
    w = [[p[i][0] * d[0][2 + j] + p[i][1] * d[1][2 + j] for j in two] for i in two]
    s = [[d[2 + i][2 + j] - (d[0][2 + i] * w[0][j] + d[1][2 + i] * w[1][j]) for j in two] for i in two]
    q = inverse_of_2(s[0][0], s[0][1], s[1][1])
    v = [[w[i][0] * q[0][j] + w[i][1] * q[1][j] for j in two] for i in two]
    m = [[None] * 4 for _ in range(4)]
    for i in two:
        for j in two:
            m[2 + i][2 + j] = q[i][j]
            m[i][2 + j] = -v[i][j]
            m[2 + j][i] = -v[i][j]
            m[i][j] = p[i][j] + v[i][0] * w[j][0] + v[i][1] * w[j][1]
    return m


def inverse_of_block(block):
    n = block.shape[0]
    lane = lax.broadcasted_iota(jnp.int32, (8, n), 1)
    sub = lax.broadcasted_iota(jnp.int32, (8, n), 0)
    tiles = [block[8 * t : 8 * t + 8, :] for t in range(n // 8)]
    four = range(4)
    for j in range(0, n, 4):
        t0, s0 = j // 8, j % 8
        cols = [[wide(t[:, j + a : j + a + 1], n) for a in four] for t in tiles]
        rows = [wide(tiles[t0][s0 + a : s0 + a + 1, :], n) for a in four]
        m = inverse_of_4([[wide(cols[t0][c][s0 + a : s0 + a + 1, :], n) for c in four] for a in four])
        inside = (lane >= j) & (lane < j + 4)
        rows = [jnp.where(inside, jnp.where(lane == j + a, 1.0, 0.0), rows[a]) for a in four]
        g = [m[a][0] * rows[0] + m[a][1] * rows[1] + (m[a][2] * rows[2] + m[a][3] * rows[3]) for a in four]
        for t in range(n // 8):
            v = jnp.where(inside, 0.0, tiles[t])
            for a in four:
                v = v - cols[t][a] * g[a]
            if t == t0:
                for a in four:
                    v = jnp.where(sub == s0 + a, g[a], v)
            tiles[t] = v
    return jnp.concatenate(tiles, axis=0)


def update_kernel(s, pr, pc, pd, cov, w, labels, cov_out, w_out, a, pcc, dd):
    y = lax.axis_index("y")
    k = lax.axis_index("k")
    h = 64
    top = s[0:4].reshape(128, 128)
    low = s[4:6].reshape(h, 128)
    end = s[6:8].reshape(h, 128)[:, 0:h]
    eye = (
        lax.broadcasted_iota(jnp.int32, (B, B), 0) == lax.broadcasted_iota(jnp.int32, (B, B), 1)
    ).astype(F32)
    a[0:128, 0:128] = 0.5 * (top + top.T)
    a[128:192, 0:128] = low
    a[0:128, 128:192] = low.T
    a[128:192, 128:192] = 0.5 * (end + end.T)
    a[...] = a[...] + eye
    for n in range(3):
        lo = h * n
        panel = a[lo : lo + h, :]
        inv = inverse_of_block(panel[:, lo : lo + h])
        g = dot(inv, panel)
        for m in range(3):
            if m != n:
                c = a[h * m : h * m + h, lo : lo + h]
                a[h * m : h * m + h, :] = a[h * m : h * m + h, :] - dot(c, g)
                a[h * m : h * m + h, lo : lo + h] = -dot(c, inv)
        a[lo : lo + h, :] = g
        a[lo : lo + h, lo : lo + h] = inv
    for r in range(16):
        pcc[F * r : F * (r + 1), :] = pc[r % 2, r // 2, 0:F, :]
    named = jnp.broadcast_to(labels[...].astype(F32), (128, B)).T
    lane = lax.broadcasted_iota(jnp.int32, (B, 128), 1).astype(F32)
    for j in range(NY):
        for q in range(8):
            at = slice(DR * q, DR * (q + 1))
            dd[at, CY * j : CY * (j + 1)] = (named[at] == lane[at] + float(CY * j)).astype(F32) - pd[q, j]
    inv = a[...]
    gain = dot(pcc[...], inv)
    cov_out[...] = cov[...] - dot(gain, pr[...].reshape(RF, B), NT)
    own = dot(pc[k, y], inv)
    w_out[...] = w[...] + dot(own, dd[...])[0:F]


def vmem(shape):
    return pltpu.VMEM(shape, F32)


def on_device(covariance, samples, labels, weights):
    in_vmem = pl.BlockSpec(memory_space=pltpu.VMEM)
    cov_t = covariance.T
    sems = lambda n: pltpu.SemaphoreType.DMA((n,))
    one = pltpu.SemaphoreType.DMA
    s, pr, pc, pd = pl.pallas_call(
        exchange_kernel,
        name="exchange",
        out_shape=(
            jax.ShapeDtypeStruct((8, SR, 128), F32),
            jax.ShapeDtypeStruct((NX, XF, B), F32),
            jax.ShapeDtypeStruct((2, NY, FP, B), F32),
            jax.ShapeDtypeStruct((8, NY, DR, CY), F32),
        ),
        in_specs=[pl.BlockSpec(memory_space=pl.ANY), in_vmem, in_vmem],
        out_specs=(in_vmem,) * 4,
        scratch_shapes=[
            vmem((CF, RF)), vmem((16 * FP, RF)), vmem((RF, 16 * FP)),
            vmem((FP, B)), vmem((NY, FP, CY)), vmem((2, NY, FP, B)), vmem((8, FP, B)), vmem((XF, B)),
            vmem((NY, FP, CY)), vmem((NX, XF, B)), vmem((NX, XF, B)), vmem((XF, B)), vmem((NZ, FP, B)),
            vmem((NZ, FP, B)), vmem((NZ, FP, B)), vmem((XF, B)),
            vmem((8, AR, 128)), vmem((8, AR, 128)), vmem((AR, 128)), vmem((NZ, AR, 128)), vmem((NY, AR, 128)),
            vmem((SR, 128)),
            one, one, sems(8), one, sems(8), sems(8), sems(4), sems(8), sems(8), sems(8), sems(8), sems(8), sems(8),
            one, sems(4), sems(8), sems(8),
        ],
        compiler_params=pltpu.CompilerParams(
            collective_id=0, has_side_effects=True, vmem_limit_bytes=40 * 2**20
        ),
    )(cov_t, samples.T, weights)
    cov_new, w_new = pl.pallas_call(
        update_kernel,
        name="update",
        out_shape=(jax.ShapeDtypeStruct((CF, RF), F32), jax.ShapeDtypeStruct((F, C), F32)),
        in_specs=[in_vmem] * 7,
        out_specs=(in_vmem,) * 2,
        scratch_shapes=[vmem((B, B)), vmem((CF, B)), vmem((B, C))],
        compiler_params=pltpu.CompilerParams(vmem_limit_bytes=40 * 2**20),
    )(s, pr, pc, pd, cov_t, weights, labels.reshape(1, B))
    return cov_new.T, w_new


def solution(mesh):
    finer = Mesh(mesh.devices.reshape(NY, NK, NX, NZ), ("y", "k", "x", "z"))
    row, col, both = ("y", "k"), ("x", "z"), ("x", "z", "y", "k")
    in_specs = (P(row, col), P(None, both), P(), P(both, None))
    out_specs = (P(row, col), P(both, None))
    return jax.shard_map(on_device, mesh=finer, in_specs=in_specs, out_specs=out_specs, check_vma=False)
```

time: 307 us -> 127 us (0.41); the launches traced: 304 us -> 127 us
  Pallas kernels: 0 us -> 123 us
  blocking collectives: 116 us -> 0 us
  waiting for transfers between devices: 81.1 us -> 0 us
  other arithmetic: 53 us -> 0 us
  between operations: 15.6 us -> 0.67 us
  matrix products: 12.2 us -> 0 us
  local copies, waits for them, and re-layouts: 14.4 us -> 3.41 us
  starting transfers between devices: 10.8 us -> 0 us
    pallas_call x0 -> x2, Pallas kernels: none -> 123 us  [the longest x1 109 us: on_device(): pl.pallas_call(exchange_kernel, name='exchange', out_shape=(jax.ShapeDtyp...]
    all_to_all x5 -> x0, blocking collectives: 116 us -> none  [the longest x2 66.4 us: sent_and_summed(): pieces = lax.all_to_all(split_up(value, dim, count), axis, 0, 0, tiled=True)]
    another operation x13 -> x0, other arithmetic: 50.2 us -> none  [the longest x7 28.7 us: on_device(): factor = jnp.linalg.cholesky(innovation)]
    all_to_all x2 -> x0, waiting for transfers between devices: 41.2 us -> none  [from_everyone(): return lax.all_to_all(copies, axis, split_axis=0, concat_axis=0, tiled=True)]
    all_gather x1 -> x0, waiting for transfers between devices: 39.9 us -> none  [from_root(): lax.all_gather(value, axis)]
    all_to_all x2 -> x0, starting transfers between devices: 10.8 us -> none  [from_everyone(): return lax.all_to_all(copies, axis, split_axis=0, concat_axis=0, tiled=True)]
    dot_general x5 -> x0, matrix products: 7.16 us -> none  [the longest x1 2.22 us: on_device(): jnp.dot(gain_piece.T, targets - predicted, precision=precise, preferred_e...]
    another operation x8 -> x0, matrix products: 5.08 us -> none  [the longest x6 4.71 us: on_device(): gain_cols = jax.scipy.linalg.cho_solve((factor, True), u_cols)]
  transfers between devices with their start and end apart: 3 -> 0, of which waited for: 3 -> 0; matrix products, arithmetic and copies ran while one was open for 1% -> 0% of each run, Pallas kernels for 0% -> 0%
where the time goes in v1:
time: 127 us
  Pallas kernels  123 us (97%)
  local copies, waits for them, and re-layouts  3.41 us (3%)
    pallas_call x1, Pallas kernels, on_device(): pl.pallas_call(exchange_kernel, name='exchange', out_shape=(jax.ShapeDtyp...  109 us
    pallas_call x1, Pallas kernels, on_device(): pl.pallas_call(update_kernel, name='update', out_shape=(jax.ShapeDtypeStr...  13.6 us
    unnamed x10, local copies, waits for them, and re-layouts  3.41 us

profile of v1, /device:TPU:1, one launch (start us, length us, event | category | flops | bytes accessed | tf_op | source)
XLA Modules:
  0.0 126.7 jit_solution(8458882953595042001)
XLA Ops:
  0.6 0.0 copy-start
  0.6 1.1 copy-done
  1.7 0.0 copy-start.1
  1.7 0.9 copy-done.1
  2.6 0.0 copy-start.3
  2.6 0.7 copy-done.3
  3.4 0.0 copy-start.2
  3.4 109.0 %exchange.1 = (f32[8,32,128]{2,1,0:T(8,128)S(1)}, f32[4,144,192]{2,1,0:T(8,128)S(1)}, f32[2,8,24,192]{3,2,1,0:T(8,128)S(1)}, f32[8,8,24,128]{3,2,1,0:T(8,128)S(1)}) custom-call(f32[288,576]{1,0:T(8,128)S(1)} %bitcast.4, f32[18,192]{1,0:T(8,128)S(1)} %bitcast.6, f32[18,1024]{1,0:T(8,128)S(1)} %copy-done.1), custom_call_target="tpu_custom_call" | custom-call | tf_op jit(solution)/shard_map/exchange/pallas_call | solution.py:376
  112.4 0.0 copy-start.4
  112.4 0.0 copy-done.2
  112.5 0.7 copy-done.4
  113.1 13.6 %update.1 = (f32[288,576]{1,0:T(8,128)}, f32[18,1024]{1,0:T(8,128)}) custom-call(f32[8,32,128]{2,1,0:T(8,128)S(1)} %get-tuple-element.8.s, f32[4,144,192]{2,1,0:T(8,128)S(1)} %get-tuple-element.9.pr, f32[2,8,24,192]{3,2,1,0:T(8,128)S(1)} %get-tuple-element.10.pc, f32[8,8,24,128]{3,2,1,0:T(8,128)S(1)} %get-tuple-element.11.pd, f32[288,576]{1,0:T(8,128)S(1)} %bitcast.5, ...), custom_call_target="tpu_custom_call" | custom-call | tf_op jit(solution)/shard_map/update/pallas_call | solution.py:401
Async XLA Ops:
  0.6 1.1 copy-start
  1.7 0.9 copy-start.1
  2.6 0.7 copy-start.3
  3.4 109.1 %copy-start.2 = (f32[18,1024]{1,0:T(8,128)S(1)}, f32[18,1024]{1,0:T(8,128)}, u32[]{:S(2)}) copy-start(f32[18,1024]{1,0:T(8,128)} %w.1) | copy-start | bytes 221188
  112.4 0.7 copy-start.4

commit v2 on v0

v2 whole, which is shorter than its diff:
```python
import functools

import jax
import jax.numpy as jnp
from jax import lax
from jax.experimental import pallas as pl
from jax.experimental.pallas import tpu as pltpu
from jax.sharding import Mesh
from jax.sharding import PartitionSpec as P

MESH = pl.DeviceIdType.MESH
HIGH = lax.Precision.HIGHEST
F32 = jnp.float32

NY, NK, NX, NZ = 8, 2, 4, 8
B = 192
F = 18
FP = 24
CF, RF = 288, 576
XF = 144
C = 1024
CY = C // NY
SR, DR = 32, 24
AR = SR + DR


def dot(a, b, dims=(((1,), (0,)), ((), ()))):
    return lax.dot_general(a, b, dims, precision=HIGH, preferred_element_type=F32)


TN = (((0,), (0,)), ((), ()))
NT = (((1,), (1,)), ((), ()))


def wide(v, n):
    return jnp.broadcast_to(v, (8, n))


def inverse_of_2(a, b, d):
    s = 1.0 / (a * d - b * b)
    return ((d * s, -(b * s)), (-(b * s), a * s))


def inverse_of_4(d):
    two = range(2)
    p = inverse_of_2(d[0][0], d[0][1], d[1][1])
    w = [[p[i][0] * d[0][2 + j] + p[i][1] * d[1][2 + j] for j in two] for i in two]
    s = [[d[2 + i][2 + j] - (d[0][2 + i] * w[0][j] + d[1][2 + i] * w[1][j]) for j in two] for i in two]
    q = inverse_of_2(s[0][0], s[0][1], s[1][1])
    v = [[w[i][0] * q[0][j] + w[i][1] * q[1][j] for j in two] for i in two]
    m = [[None] * 4 for _ in range(4)]
    for i in two:
        for j in two:
            m[2 + i][2 + j] = q[i][j]
            m[i][2 + j] = -v[i][j]
            m[2 + j][i] = -v[i][j]
            m[i][j] = p[i][j] + v[i][0] * w[j][0] + v[i][1] * w[j][1]
    return m


def inverse_of_block(block):
    n = block.shape[0]
    lane = lax.broadcasted_iota(jnp.int32, (8, n), 1)
    sub = lax.broadcasted_iota(jnp.int32, (8, n), 0)
    tiles = [block[8 * t : 8 * t + 8, :] for t in range(n // 8)]
    four = range(4)
    for j in range(0, n, 4):
        t0, s0 = j // 8, j % 8
        cols = [[wide(t[:, j + a : j + a + 1], n) for a in four] for t in tiles]
        rows = [wide(tiles[t0][s0 + a : s0 + a + 1, :], n) for a in four]
        m = inverse_of_4([[wide(cols[t0][c][s0 + a : s0 + a + 1, :], n) for c in four] for a in four])
        inside = (lane >= j) & (lane < j + 4)
        rows = [jnp.where(inside, jnp.where(lane == j + a, 1.0, 0.0), rows[a]) for a in four]
        g = [m[a][0] * rows[0] + m[a][1] * rows[1] + (m[a][2] * rows[2] + m[a][3] * rows[3]) for a in four]
        for t in range(n // 8):
            v = jnp.where(inside, 0.0, tiles[t])
            for a in four:
                v = v - cols[t][a] * g[a]
            if t == t0:
                for a in four:
                    v = jnp.where(sub == s0 + a, g[a], v)
            tiles[t] = v
    return jnp.concatenate(tiles, axis=0)


def pivot_block(a, h, n):
    lo = h * n
    panel = a[lo : lo + h, :]
    inv = inverse_of_block(panel[:, lo : lo + h])
    g = dot(inv, panel)
    for m in range(a.shape[0] // h):
        if m != n:
            c = a[h * m : h * m + h, lo : lo + h]
            a[h * m : h * m + h, :] = a[h * m : h * m + h, :] - dot(c, g)
            a[h * m : h * m + h, lo : lo + h] = -dot(c, inv)
    a[lo : lo + h, :] = g
    a[lo : lo + h, lo : lo + h] = inv


def exchange_kernel(
    cov, xin, win,
    inv_out, pr_out, pc_out, pd_out,
    s_out, rt, rtp, rp, xpad, wst, xg, x8, x8c, wg, ts, tr, tx, tp, tzr, pz, prc,
    ar, arr, a1, azr, ayr, asum,
    lsem, ssem, s_xy, s_xk, s_xf, s_x8, s_w, s_t, s_ar, s_tz, s_az, s_ay, s_pz, s_pf, s_pc, s_pck, s_px, s_s, s_d, s_dk,
):
    y, k, x, z = (lax.axis_index(a) for a in ("y", "k", "x", "z"))
    col = NZ * x + z
    row = 2 * y + k

    def at(yy=None, kk=None, xx=None, zz=None):
        ids = {}
        for name, v in (("y", yy), ("k", kk), ("x", xx), ("z", zz)):
            if v is not None:
                ids[name] = v
        return ids

    def other(v, d, n):
        return lax.rem(v + d, n)

    sent, coming = [], {}

    def send(src, dst, sem, to, slot=None, expect=True):
        land = sem if slot is None else sem.at[slot]
        cp = pltpu.make_async_remote_copy(src, dst, ssem, land, device_id=to, device_id_type=MESH)
        cp.start()
        sent.append(cp)
        if expect:
            coming[id(sem), slot] = src, land

    def got(sem, *slots):
        for slot in slots or (None,):
            src, land = coming.pop((id(sem), slot))
            pltpu.make_async_copy(src, src, land).wait()

    fy, fk, fx, fi = col // 4, (col // 2) % 2, 2 * (col % 2) + row // 8, row % 8
    pcol = 2 * row + x // 2
    gy, gk, gx, gz = 4 * (x % 2) + z // 2, z % 2, pcol // NZ, pcol % NZ
    is_own = (fy == y) & (fk == k) & (fx == x) & (fi == z)

    barrier = pltpu.get_barrier_semaphore()

    def tell(to):
        pl.semaphore_signal(barrier, inc=1, device_id=to, device_id_type=MESH)

    for d in range(1, NY):
        tell(at(yy=other(y, d, NY)))
    for d in range(1, NZ):
        tell(at(zz=other(z, d, NZ)))
    for d in range(1, 8):
        tell(at(xx=other(x, d // 2, NX), kk=other(k, d % 2, NK)))

    @pl.when(jnp.logical_not(is_own))
    def _():
        tell(at(gy, gk, gx, gz))
        tell(at(fy, fk, fx, fi))

    load = pltpu.make_async_copy(cov, rt, lsem)
    load.start()
    xpad[...] = jnp.zeros_like(xpad)
    xpad[0:F, :] = xin[...]
    xg[k, y] = xpad[...]
    wst[...] = jnp.zeros_like(wst)
    for j in range(NY):
        wst[j, 0:F, :] = win[:, CY * j : CY * (j + 1)]
    wg[y] = wst[y]
    load.wait()
    rtp[...] = jnp.zeros_like(rtp)
    for q in range(16):
        r = 2 * (q % 8) + q // 8
        rtp[FP * q : FP * q + F, :] = rt[F * r : F * r + F, :]
    rp[...] = rtp[...].T

    pl.semaphore_wait(barrier, 7 + 7 + 7 + 2 - 2 * is_own.astype(jnp.int32))

    for d in range(1, NY):
        send(xpad, xg.at[k, y], s_xy, at(yy=other(y, d, NY)), d)

    def send_far(src, dst, sem, to):
        @pl.when(is_own)
        def _():
            pltpu.make_async_copy(src, dst, sem).start()

        @pl.when(jnp.logical_not(is_own))
        def _():
            pltpu.make_async_remote_copy(src, dst, ssem, sem, device_id=to, device_id_type=MESH).start()

        coming[id(sem), None] = src, sem

    send_far(xpad, x8.at[fi], s_xf, at(fy, fk, fx, fi))

    got(s_xy, *range(1, NY))
    send(xg.at[k], xg.at[k], s_xk, at(kk=1 - k))
    for d in range(1, NY):
        ty = other(y, d, NY)
        send(wst.at[ty], wg.at[y], s_w, at(yy=ty), d)
    got(s_xk)
    xct = xg[...].reshape(2 * NY * FP, B)
    for d in (2, 1, 3, 0):
        tx_ = other(x, d, NX)
        ts[d] = dot(rp[pl.ds(pl.multiple_of(XF * tx_, 16), XF), :], xct)
        if d:
            send(ts.at[d], tr.at[d], s_t, at(xx=tx_), d)
    got(s_xf)
    for d in range(1, NZ):
        send(x8.at[z], x8.at[z], s_x8, at(zz=other(z, d, NZ)), d)
    got(s_w, *range(1, NY))
    part = dot(xg[k].reshape(NY * FP, B), wg[...].reshape(NY * FP, CY), TN)
    for q in range(8):
        ar[q, SR:AR, :] = part[DR * q : DR * (q + 1), :]
    got(s_x8, *range(1, 8))
    for i in range(8):
        x8c[F * i : F * (i + 1), :] = x8[i, 0:F, :]
    got(s_t, *range(1, NX))
    tx[...] = ts[0] + tr[1] + tr[2] + tr[3]
    inner = dot(x8c[...], tx[...], TN)
    for q in range(4):
        ar[q, 0:SR, :] = inner[SR * q : SR * (q + 1), 0:128]
    for q in range(2):
        ar[4 + q, 0:SR, :] = inner[128 + SR * q : 128 + SR * (q + 1), 0:128]
        ar[6 + q, 0:SR, :] = jnp.zeros((SR, 128), F32)
        ar[6 + q, 0:SR, 0:64] = inner[128 + SR * q : 128 + SR * (q + 1), 128:192]
    for d in range(1, 8):
        tx_, tk_ = other(x, d // 2, NX), other(k, d % 2, NK)
        send(ar.at[2 * tx_ + tk_], arr.at[d], s_ar, at(xx=tx_, kk=tk_), d)
    tp[...] = jnp.zeros_like(tp)
    for i in range(8):
        tp[i, 0:F, :] = tx[F * i : F * (i + 1), :]
    for d in range(1, NZ):
        tz = other(z, d, NZ)
        send(tp.at[tz], tzr.at[d], s_tz, at(zz=tz), d)

    got(s_ar, *range(1, 8))
    q_own = 2 * x + k
    total = ar[q_own]
    for d in range(1, 8):
        total = total + arr[d]
    a1[...] = total
    for d in range(1, NZ):
        send(a1, azr.at[d], s_az, at(zz=other(z, d, NZ)), d)

    got(s_az, *range(1, NZ))
    total = a1[...]
    for d in range(1, NZ):
        total = total + azr[d]
    ayr[y] = total
    for d in range(1, NY):
        send(ayr.at[y], ayr.at[y], s_ay, at(yy=other(y, d, NY)), d)

    got(s_tz, *range(1, NZ))
    piece = tp[z]
    for d in range(1, NZ):
        piece = piece + tzr[d]
    pz[z] = piece
    for d in range(1, NZ):
        send(pz.at[z], pz.at[z], s_pz, at(zz=other(z, d, NZ)), d)
    send_far(pz.at[z], pc_out.at[gk, gy], s_pf, at(gy, gk, gx, gz))

    got(s_ay, *range(1, NY))
    total = ayr[0, 0:SR, :]
    for j in range(1, NY):
        total = total + ayr[j, 0:SR, :]
    asum[...] = total
    s_out[q_own] = total
    for d in range(1, 8):
        send(asum, s_out.at[q_own], s_s, at(xx=other(x, d // 2, NX), kk=other(k, d % 2, NK)), d)
    got(s_pz, *range(1, NZ))
    for i in range(8):
        prc[F * i : F * (i + 1), :] = pz[i, 0:F, :]
    pr_out[x] = prc[...]
    for d in range(1, NX):
        send(prc, pr_out.at[x], s_px, at(xx=other(x, d, NX)), d)
    got(s_pf)
    for d in range(1, NY):
        send(pc_out.at[k, y], pc_out.at[k, y], s_pc, at(yy=other(y, d, NY)), d)
    pd_out[k, x] = ayr[:, SR:AR, :]
    for d in range(1, NX):
        send(pd_out.at[k, x], pd_out.at[k, x], s_d, at(xx=other(x, d, NX)), d)

    got(s_s, *range(1, 8))
    h = 64
    top = s_out[0:4].reshape(128, 128)
    low = s_out[4:6].reshape(h, 128)
    end = s_out[6:8].reshape(h, 128)[:, 0:h]
    eye = (
        lax.broadcasted_iota(jnp.int32, (B, B), 0) == lax.broadcasted_iota(jnp.int32, (B, B), 1)
    ).astype(F32)
    inv_out[0:128, 0:128] = 0.5 * (top + top.T)
    inv_out[128:192, 0:128] = low
    inv_out[0:128, 128:192] = low.T
    inv_out[128:192, 128:192] = 0.5 * (end + end.T)
    inv_out[...] = inv_out[...] + eye
    for n in range(3):
        pivot_block(inv_out, h, n)
        if n == 0:
            got(s_pc, *range(1, 8))
            send(pc_out.at[k], pc_out.at[k], s_pck, at(kk=1 - k))
            got(s_d, *range(1, NX))
            send(pd_out.at[k], pd_out.at[k], s_dk, at(kk=1 - k))
    got(s_px, *range(1, NX))
    got(s_pck)
    got(s_dk)
    for cp in sent:
        cp.wait_send()

    @pl.when(jnp.logical_not(is_own))
    def _():
        pltpu.make_async_copy(xpad, xpad, ssem).wait()
        pltpu.make_async_copy(xpad, xpad, ssem).wait()


def update_kernel(inv, pr, pc, pd, cov, w, labels, cov_out, w_out, pcc, dd):
    y = lax.axis_index("y")
    k = lax.axis_index("k")
    for r in range(16):
        pcc[F * r : F * (r + 1), :] = pc[r % 2, r // 2, 0:F, :]
    named = jnp.broadcast_to(labels[...].astype(F32), (128, B)).T
    lane = lax.broadcasted_iota(jnp.int32, (B, 128), 1).astype(F32)
    for j in range(NY):
        for q in range(8):
            at = slice(DR * q, DR * (q + 1))
            dd[at, CY * j : CY * (j + 1)] = (named[at] == lane[at] + float(CY * j)).astype(F32) - pd[q % 2, q // 2, j]
    gain = dot(pcc[...], inv[...])
    cov_out[...] = cov[...] - dot(gain, pr[...].reshape(RF, B), NT)
    own = dot(pc[k, y], inv[...])
    w_out[...] = w[...] + dot(own, dd[...])[0:F]


def vmem(shape):
    return pltpu.VMEM(shape, F32)


def on_device(covariance, samples, labels, weights):
    in_vmem = pl.BlockSpec(memory_space=pltpu.VMEM)
    cov_t = covariance.T
    sems = lambda n: pltpu.SemaphoreType.DMA((n,))
    one = pltpu.SemaphoreType.DMA
    inv, pr, pc, pd = pl.pallas_call(
        exchange_kernel,
        name="exchange",
        out_shape=(
            jax.ShapeDtypeStruct((B, B), F32),
            jax.ShapeDtypeStruct((NX, XF, B), F32),
            jax.ShapeDtypeStruct((2, NY, FP, B), F32),
            jax.ShapeDtypeStruct((2, NX, NY, DR, CY), F32),
        ),
        in_specs=[pl.BlockSpec(memory_space=pl.ANY), in_vmem, in_vmem],
        out_specs=(in_vmem,) * 4,
        scratch_shapes=[
            vmem((8, SR, 128)), vmem((CF, RF)), vmem((16 * FP, RF)), vmem((RF, 16 * FP)),
            vmem((FP, B)), vmem((NY, FP, CY)), vmem((2, NY, FP, B)), vmem((8, FP, B)), vmem((XF, B)),
            vmem((NY, FP, CY)), vmem((NX, XF, B)), vmem((NX, XF, B)), vmem((XF, B)), vmem((NZ, FP, B)),
            vmem((NZ, FP, B)), vmem((NZ, FP, B)), vmem((XF, B)),
            vmem((8, AR, 128)), vmem((8, AR, 128)), vmem((AR, 128)), vmem((NZ, AR, 128)), vmem((NY, AR, 128)),
            vmem((SR, 128)),
            one, one, sems(8), one, one, sems(8), sems(8), sems(4), sems(8), sems(8), sems(8), sems(8), sems(8), one, sems(8),
            one, sems(4), sems(8), sems(4), one,
        ],
        compiler_params=pltpu.CompilerParams(
            collective_id=0, has_side_effects=True, vmem_limit_bytes=40 * 2**20
        ),
    )(cov_t, samples.T, weights)
    cov_new, w_new = pl.pallas_call(
        update_kernel,
        name="update",
        out_shape=(jax.ShapeDtypeStruct((CF, RF), F32), jax.ShapeDtypeStruct((F, C), F32)),
        in_specs=[in_vmem] * 7,
        out_specs=(in_vmem,) * 2,
        scratch_shapes=[vmem((CF, B)), vmem((B, C))],
        compiler_params=pltpu.CompilerParams(vmem_limit_bytes=40 * 2**20),
    )(inv, pr, pc, pd, cov_t, weights, labels.reshape(1, B))
    return cov_new.T, w_new


def solution(mesh):
    finer = Mesh(mesh.devices.reshape(NY, NK, NX, NZ), ("y", "k", "x", "z"))
    row, col, both = ("y", "k"), ("x", "z"), ("x", "z", "y", "k")
    in_specs = (P(row, col), P(None, both), P(), P(both, None))
    out_specs = (P(row, col), P(both, None))
    return jax.shard_map(on_device, mesh=finer, in_specs=in_specs, out_specs=out_specs, check_vma=False)
```

time: 307 us -> 85.2 us (0.28)
  the two profiles are of different devices: /device:TPU:1 before, /device:TPU:16 now
where the time goes in v2:
time: 85.2 us; the launch traced here: 85 us
  Pallas kernels  80.9 us (95%)
  local copies, waits for them, and re-layouts  3.41 us (4%)
    pallas_call x1, Pallas kernels, on_device(): pl.pallas_call(exchange_kernel, name='exchange', out_shape=(jax.ShapeDtyp...  78.3 us
    unnamed x10, local copies, waits for them, and re-layouts  3.41 us
    pallas_call x1, Pallas kernels, on_device(): pl.pallas_call(update_kernel, name='update', out_shape=(jax.ShapeDtypeStr...  2.54 us

profile of v2, /device:TPU:16, one launch (start us, length us, event | category | flops | bytes accessed | tf_op | source)
XLA Modules:
  0.0 85.0 jit_solution(13353513126928289579)
XLA Ops:
  0.6 0.0 copy-start
  0.6 1.1 %copy-done = f32[576,288]{0,1:T(8,128)S(1)} copy-done((f32[576,288]{0,1:T(8,128)S(1)}, f32[576,288]{0,1:T(8,128)}, u32[]{:S(2)}) %copy-start) | copy-done | bytes 663576
  1.7 0.0 copy-start.1
  1.7 0.9 %copy-done.1 = f32[18,1024]{1,0:T(8,128)S(1)} copy-done((f32[18,1024]{1,0:T(8,128)S(1)}, f32[18,1024]{1,0:T(8,128)}, u32[]{:S(2)}) %copy-start.1) | copy-done | bytes 73752
  2.6 0.0 copy-start.3
  2.6 0.7 copy-done.3
  3.4 0.0 copy-start.2
  3.4 78.3 %exchange.1 = (f32[192,192]{1,0:T(8,128)S(1)}, f32[4,144,192]{2,1,0:T(8,128)S(1)}, f32[2,8,24,192]{3,2,1,0:T(8,128)S(1)}, f32[2,4,8,24,128]{4,3,2,1,0:T(8,128)S(1)}) custom-call(f32[288,576]{1,0:T(8,128)S(1)} %bitcast.4, f32[18,192]{1,0:T(8,128)S(1)} %bitcast.6, f32[18,1024]{1,0:T(8,128)S(1)} %copy-done.1), custom_call_target="tpu_custom_call" | custom-call | tf_op jit(solution)/shard_map/exchange/pallas_call | solution.py:338
  81.7 0.0 copy-start.4
  81.7 0.0 copy-done.2
  81.8 0.7 copy-done.4
  82.4 2.5 %update.1 = (f32[288,576]{1,0:T(8,128)}, f32[18,1024]{1,0:T(8,128)}) custom-call(f32[192,192]{1,0:T(8,128)S(1)} %get-tuple-element.8.inv, f32[4,144,192]{2,1,0:T(8,128)S(1)} %get-tuple-element.9.pr, f32[2,8,24,192]{3,2,1,0:T(8,128)S(1)} %get-tuple-element.10.pc, f32[2,4,8,24,128]{4,3,2,1,0:T(8,128)S(1)} %get-tuple-element.11.pd, f32[288,576]{1,0:T(8,128)S(1)} %bitcast.5, ...), custom_call_target="tpu_custom_call" | custom-call | tf_op jit(solution)/shard_map/update/pallas_call | solution.py:363
Async XLA Ops:
  0.6 1.1 %copy-start = (f32[576,288]{0,1:T(8,128)S(1)}, f32[576,288]{0,1:T(8,128)}, u32[]{:S(2)}) copy-start(f32[576,288]{0,1:T(8,128)} %param.4) | copy-start | bytes 1990660
  1.7 0.9 %copy-start.1 = (f32[18,1024]{1,0:T(8,128)S(1)}, f32[18,1024]{1,0:T(8,128)}, u32[]{:S(2)}) copy-start(f32[18,1024]{1,0:T(8,128)} %w.1) | copy-start | bytes 221188
  2.6 0.7 copy-start.3
  3.4 78.4 %copy-start.2 = (f32[18,1024]{1,0:T(8,128)S(1)}, f32[18,1024]{1,0:T(8,128)}, u32[]{:S(2)}) copy-start(f32[18,1024]{1,0:T(8,128)} %w.1) | copy-start | bytes 221188
  81.7 0.7 copy-start.4

commit v3 on v2

--- a/solution.py
+++ b/solution.py
@@ -16,12 +16,13 @@
 B = 192
 F = 18
 FP = 24
+PP = 32
 CF, RF = 288, 576
 XF = 144
 C = 1024
 CY = C // NY
+XR = XF + XF // 2
 SR, DR = 32, 24
-AR = SR + DR
 
 
 def dot(a, b, dims=(((1,), (0,)), ((), ()))):
@@ -83,6 +84,18 @@
     return jnp.concatenate(tiles, axis=0)
 
 
+def fold(ref, at, rows, row):
+    ref[(*at, slice(0, F), slice(None))] = rows[row : row + F, 0:128]
+    ref[(*at, slice(F, F + 9), slice(0, 64))] = rows[row : row + 9, 128:192]
+    ref[(*at, slice(F, F + 9), slice(64, 128))] = rows[row + 9 : row + F, 128:192]
+
+
+def unfold(ref, at, row, piece):
+    ref[(*at, slice(row, row + F), slice(0, 128))] = piece[0:F]
+    ref[(*at, slice(row, row + 9), slice(128, 192))] = piece[F : F + 9, 0:64]
+    ref[(*at, slice(row + 9, row + F), slice(128, 192))] = piece[F : F + 9, 64:128]
+
+
 def pivot_block(a, h, n):
     lo = h * n
     panel = a[lo : lo + h, :]
@@ -99,10 +112,11 @@
 
 def exchange_kernel(
     cov, xin, win,
-    inv_out, pr_out, pc_out, pd_out,
-    s_out, rt, rtp, rp, xpad, wst, xg, x8, x8c, wg, ts, tr, tx, tp, tzr, pz, prc,
-    ar, arr, a1, azr, ayr, asum,
+    inv_out, pr_out, pc_out, pd_out, rt, wt,
+    s_out, xt, rtp, rp, xpad, wst, xg, xu, x8, x8c, wg, ts, tr, tx, tp, tzr, pz, prc,
+    ar, arr, a1, azr, ayr, asum, dr, drr, d1, dzr, dyr,
     lsem, ssem, s_xy, s_xk, s_xf, s_x8, s_w, s_t, s_ar, s_tz, s_az, s_ay, s_pz, s_pf, s_pc, s_pck, s_px, s_s, s_d, s_dk,
+    s_dx, s_dz, s_dy,
 ):
     y, k, x, z = (lax.axis_index(a) for a in ("y", "k", "x", "z"))
     col = NZ * x + z
@@ -155,16 +169,21 @@
         tell(at(gy, gk, gx, gz))
         tell(at(fy, fk, fx, fi))
 
-    load = pltpu.make_async_copy(cov, rt, lsem)
-    load.start()
+    loads = [pltpu.make_async_copy(f, t, lsem.at[i]) for i, (f, t) in enumerate(((xin, xt), (win, wt), (cov, rt)))]
+    for load in loads:
+        load.start()
     xpad[...] = jnp.zeros_like(xpad)
-    xpad[0:F, :] = xin[...]
+    xu[...] = jnp.zeros_like(xu)
+    tp[...] = jnp.zeros_like(tp)
+    wst[...] = jnp.zeros_like(wst)
+    loads[0].wait()
+    fold(xpad, (), xt, 0)
     xg[k, y] = xpad[...]
-    wst[...] = jnp.zeros_like(wst)
+    loads[1].wait()
     for j in range(NY):
-        wst[j, 0:F, :] = win[:, CY * j : CY * (j + 1)]
+        wst[j, 0:F, :] = wt[:, CY * j : CY * (j + 1)]
     wg[y] = wst[y]
-    load.wait()
+    loads[2].wait()
     rtp[...] = jnp.zeros_like(rtp)
     for q in range(16):
         r = 2 * (q % 8) + q // 8
@@ -194,38 +213,53 @@
     for d in range(1, NY):
         ty = other(y, d, NY)
         send(wst.at[ty], wg.at[y], s_w, at(yy=ty), d)
+    for j in range(NY):
+        unfold(xu, (k,), FP * j, xg[k, j])
     got(s_xk)
-    xct = xg[...].reshape(2 * NY * FP, B)
+    for j in range(NY):
+        unfold(xu, (1 - k,), FP * j, xg[1 - k, j])
+    xct = xu[...].reshape(2 * NY * FP, B)
     for d in (2, 1, 3, 0):
         tx_ = other(x, d, NX)
-        ts[d] = dot(rp[pl.ds(pl.multiple_of(XF * tx_, 16), XF), :], xct)
+        t = dot(rp[pl.ds(pl.multiple_of(XF * tx_, 16), XF), :], xct)
+        ts[d, 0:XF, :] = t[:, 0:128]
+        for i in range(8):
+            ts[d, XF + 9 * i : XF + 9 * i + 9, 0:64] = t[F * i : F * i + 9, 128:192]
+            ts[d, XF + 9 * i : XF + 9 * i + 9, 64:128] = t[F * i + 9 : F * i + F, 128:192]
         if d:
             send(ts.at[d], tr.at[d], s_t, at(xx=tx_), d)
     got(s_xf)
     for d in range(1, NZ):
         send(x8.at[z], x8.at[z], s_x8, at(zz=other(z, d, NZ)), d)
     got(s_w, *range(1, NY))
-    part = dot(xg[k].reshape(NY * FP, B), wg[...].reshape(NY * FP, CY), TN)
+    part = dot(xu[k], wg[...].reshape(NY * FP, CY), TN)
     for q in range(8):
-        ar[q, SR:AR, :] = part[DR * q : DR * (q + 1), :]
+        dr[q] = part[DR * q : DR * (q + 1), :]
     got(s_x8, *range(1, 8))
     for i in range(8):
-        x8c[F * i : F * (i + 1), :] = x8[i, 0:F, :]
+        unfold(x8c, (), F * i, x8[i])
     got(s_t, *range(1, NX))
-    tx[...] = ts[0] + tr[1] + tr[2] + tr[3]
+    ts[0] = ts[0] + tr[1] + tr[2] + tr[3]
+    tx[:, 0:128] = ts[0, 0:XF, :]
+    for i in range(8):
+        tx[F * i : F * i + 9, 128:192] = ts[0, XF + 9 * i : XF + 9 * i + 9, 0:64]
+        tx[F * i + 9 : F * i + F, 128:192] = ts[0, XF + 9 * i : XF + 9 * i + 9, 64:128]
     inner = dot(x8c[...], tx[...], TN)
     for q in range(4):
-        ar[q, 0:SR, :] = inner[SR * q : SR * (q + 1), 0:128]
+        ar[q] = inner[SR * q : SR * (q + 1), 0:128]
     for q in range(2):
-        ar[4 + q, 0:SR, :] = inner[128 + SR * q : 128 + SR * (q + 1), 0:128]
-        ar[6 + q, 0:SR, :] = jnp.zeros((SR, 128), F32)
-        ar[6 + q, 0:SR, 0:64] = inner[128 + SR * q : 128 + SR * (q + 1), 128:192]
+        ar[4 + q] = inner[128 + SR * q : 128 + SR * (q + 1), 0:128]
+        ar[6 + q] = jnp.zeros((SR, 128), F32)
+        ar[6 + q, :, 0:64] = inner[128 + SR * q : 128 + SR * (q + 1), 128:192]
     for d in range(1, 8):
         tx_, tk_ = other(x, d // 2, NX), other(k, d % 2, NK)
         send(ar.at[2 * tx_ + tk_], arr.at[d], s_ar, at(xx=tx_, kk=tk_), d)
-    tp[...] = jnp.zeros_like(tp)
+    for d in range(1, 8):
+        tx_, tk_ = other(x, d // 2, NX), other(k, d % 2, NK)
+        send(dr.at[2 * tx_ + tk_], drr.at[d], s_dx, at(xx=tx_, kk=tk_), d)
     for i in range(8):
-        tp[i, 0:F, :] = tx[F * i : F * (i + 1), :]
+        tp[i, 0:F, :] = ts[0, F * i : F * (i + 1), :]
+        tp[i, F : F + 9, :] = ts[0, XF + 9 * i : XF + 9 * i + 9, :]
     for d in range(1, NZ):
         tz = other(z, d, NZ)
         send(tp.at[tz], tzr.at[d], s_tz, at(zz=tz), d)
@@ -238,6 +272,13 @@
     a1[...] = total
     for d in range(1, NZ):
         send(a1, azr.at[d], s_az, at(zz=other(z, d, NZ)), d)
+    got(s_dx, *range(1, 8))
+    total = dr[q_own]
+    for d in range(1, 8):
+        total = total + drr[d]
+    d1[...] = total
+    for d in range(1, NZ):
+        send(d1, dzr.at[d], s_dz, at(zz=other(z, d, NZ)), d)
 
     got(s_az, *range(1, NZ))
     total = a1[...]
@@ -247,6 +288,13 @@
     for d in range(1, NY):
         send(ayr.at[y], ayr.at[y], s_ay, at(yy=other(y, d, NY)), d)
 
+    got(s_dz, *range(1, NZ))
+    total = d1[...]
+    for d in range(1, NZ):
+        total = total + dzr[d]
+    dyr[y] = total
+    for d in range(1, NY):
+        send(dyr.at[y], dyr.at[y], s_dy, at(yy=other(y, d, NY)), d)
     got(s_tz, *range(1, NZ))
     piece = tp[z]
     for d in range(1, NZ):
@@ -257,9 +305,9 @@
     send_far(pz.at[z], pc_out.at[gk, gy], s_pf, at(gy, gk, gx, gz))
 
     got(s_ay, *range(1, NY))
-    total = ayr[0, 0:SR, :]
+    total = ayr[0]
     for j in range(1, NY):
-        total = total + ayr[j, 0:SR, :]
+        total = total + ayr[j]
     asum[...] = total
     s_out[q_own] = total
     for d in range(1, 8):
@@ -267,13 +315,15 @@
     got(s_pz, *range(1, NZ))
     for i in range(8):
         prc[F * i : F * (i + 1), :] = pz[i, 0:F, :]
+        prc[XF + 9 * i : XF + 9 * i + 9, :] = pz[i, F : F + 9, :]
     pr_out[x] = prc[...]
     for d in range(1, NX):
         send(prc, pr_out.at[x], s_px, at(xx=other(x, d, NX)), d)
     got(s_pf)
     for d in range(1, NY):
         send(pc_out.at[k, y], pc_out.at[k, y], s_pc, at(yy=other(y, d, NY)), d)
-    pd_out[k, x] = ayr[:, SR:AR, :]
+    got(s_dy, *range(1, NY))
+    pd_out[k, x] = dyr[...]
     for d in range(1, NX):
         send(pd_out.at[k, x], pd_out.at[k, x], s_d, at(xx=other(x, d, NX)), d)
 
@@ -309,11 +359,18 @@
         pltpu.make_async_copy(xpad, xpad, ssem).wait()
 
 
-def update_kernel(inv, pr, pc, pd, cov, w, labels, cov_out, w_out, pcc, dd):
+def update_kernel(inv, pr, pc, pd, cov, w, labels, cov_out, w_out, pcc, dd, prc, pco):
     y = lax.axis_index("y")
     k = lax.axis_index("k")
     for r in range(16):
-        pcc[F * r : F * (r + 1), :] = pc[r % 2, r // 2, 0:F, :]
+        unfold(pcc, (), F * r, pc[r % 2, r // 2])
+    for j in range(NX):
+        prc[j, :, 0:128] = pr[j, 0:XF, :]
+        for i in range(8):
+            prc[j, F * i : F * i + 9, 128:192] = pr[j, XF + 9 * i : XF + 9 * i + 9, 0:64]
+            prc[j, F * i + 9 : F * i + F, 128:192] = pr[j, XF + 9 * i : XF + 9 * i + 9, 64:128]
+    pco[...] = jnp.zeros_like(pco)
+    unfold(pco, (), 0, pc[k, y])
     named = jnp.broadcast_to(labels[...].astype(F32), (128, B)).T
     lane = lax.broadcasted_iota(jnp.int32, (B, 128), 1).astype(F32)
     for j in range(NY):
@@ -321,8 +378,8 @@
             at = slice(DR * q, DR * (q + 1))
             dd[at, CY * j : CY * (j + 1)] = (named[at] == lane[at] + float(CY * j)).astype(F32) - pd[q % 2, q // 2, j]
     gain = dot(pcc[...], inv[...])
-    cov_out[...] = cov[...] - dot(gain, pr[...].reshape(RF, B), NT)
-    own = dot(pc[k, y], inv[...])
+    cov_out[...] = cov[...] - dot(gain, prc[...].reshape(RF, B), NT)
+    own = dot(pco[...], inv[...])
     w_out[...] = w[...] + dot(own, dd[...])[0:F]
 
 
@@ -335,26 +392,26 @@
     cov_t = covariance.T
     sems = lambda n: pltpu.SemaphoreType.DMA((n,))
     one = pltpu.SemaphoreType.DMA
-    inv, pr, pc, pd = pl.pallas_call(
+    inv, pr, pc, pd, cov_in, w_in = pl.pallas_call(
         exchange_kernel,
         name="exchange",
-        out_shape=(
-            jax.ShapeDtypeStruct((B, B), F32),
-            jax.ShapeDtypeStruct((NX, XF, B), F32),
-            jax.ShapeDtypeStruct((2, NY, FP, B), F32),
-            jax.ShapeDtypeStruct((2, NX, NY, DR, CY), F32),
+        out_shape=tuple(
+            jax.ShapeDtypeStruct(shape, F32)
+            for shape in ((B, B), (NX, XR, 128), (2, NY, PP, 128), (2, NX, NY, DR, CY), (CF, RF), (F, C))
         ),
-        in_specs=[pl.BlockSpec(memory_space=pl.ANY), in_vmem, in_vmem],
-        out_specs=(in_vmem,) * 4,
+        in_specs=[pl.BlockSpec(memory_space=pltpu.HBM)] * 3,
+        out_specs=(in_vmem,) * 6,
         scratch_shapes=[
-            vmem((8, SR, 128)), vmem((CF, RF)), vmem((16 * FP, RF)), vmem((RF, 16 * FP)),
-            vmem((FP, B)), vmem((NY, FP, CY)), vmem((2, NY, FP, B)), vmem((8, FP, B)), vmem((XF, B)),
-            vmem((NY, FP, CY)), vmem((NX, XF, B)), vmem((NX, XF, B)), vmem((XF, B)), vmem((NZ, FP, B)),
-            vmem((NZ, FP, B)), vmem((NZ, FP, B)), vmem((XF, B)),
-            vmem((8, AR, 128)), vmem((8, AR, 128)), vmem((AR, 128)), vmem((NZ, AR, 128)), vmem((NY, AR, 128)),
+            vmem((8, SR, 128)), vmem((F, B)), vmem((16 * FP, RF)), vmem((RF, 16 * FP)),
+            vmem((PP, 128)), vmem((NY, FP, CY)), vmem((2, NY, PP, 128)), vmem((2, NY * FP, B)),
+            vmem((8, PP, 128)), vmem((XF, B)), vmem((NY, FP, CY)),
+            vmem((NX, XR, 128)), vmem((NX, XR, 128)), vmem((XF, B)), vmem((NZ, PP, 128)),
+            vmem((NZ, PP, 128)), vmem((NZ, PP, 128)), vmem((XR, 128)),
+            vmem((8, SR, 128)), vmem((8, SR, 128)), vmem((SR, 128)), vmem((NZ, SR, 128)), vmem((NY, SR, 128)),
             vmem((SR, 128)),
-            one, one, sems(8), one, one, sems(8), sems(8), sems(4), sems(8), sems(8), sems(8), sems(8), sems(8), one, sems(8),
-            one, sems(4), sems(8), sems(4), one,
+            vmem((8, DR, 128)), vmem((8, DR, 128)), vmem((DR, 128)), vmem((NZ, DR, 128)), vmem((NY, DR, 128)),
+            sems(3), one, sems(8), one, one, sems(8), sems(8), sems(4), sems(8), sems(8), sems(8), sems(8), sems(8),
+            one, sems(8), one, sems(4), sems(8), sems(4), one, sems(8), sems(8), sems(8),
         ],
         compiler_params=pltpu.CompilerParams(
             collective_id=0, has_side_effects=True, vmem_limit_bytes=40 * 2**20
@@ -366,9 +423,9 @@
         out_shape=(jax.ShapeDtypeStruct((CF, RF), F32), jax.ShapeDtypeStruct((F, C), F32)),
         in_specs=[in_vmem] * 7,
         out_specs=(in_vmem,) * 2,
-        scratch_shapes=[vmem((CF, B)), vmem((B, C))],
+        scratch_shapes=[vmem((CF, B)), vmem((B, C)), vmem((NX, XF, B)), vmem((FP, B))],
         compiler_params=pltpu.CompilerParams(vmem_limit_bytes=40 * 2**20),
-    )(inv, pr, pc, pd, cov_t, weights, labels.reshape(1, B))
+    )(inv, pr, pc, pd, cov_in, w_in, labels.reshape(1, B))
     return cov_new.T, w_new
 
 

time: 85.2 us -> 76.7 us (0.900)
  the two profiles are of different devices: /device:TPU:16 before, /device:TPU:1 now
where the time goes in v3:
time: 76.7 us; the launch traced here: 76.5 us
  Pallas kernels  72.4 us (94%)
  local copies, waits for them, and re-layouts  3.41 us (4%)
    pallas_call x1, Pallas kernels, on_device(): pl.pallas_call(exchange_kernel, name='exchange', out_shape=tuple((jax.Sha...  69.8 us
    unnamed x8, local copies, waits for them, and re-layouts  3.41 us
    pallas_call x1, Pallas kernels, on_device(): pl.pallas_call(update_kernel, name='update', out_shape=(jax.ShapeDtypeStr...  2.66 us

profile of v3, /device:TPU:1, one launch (start us, length us, event | category | flops | bytes accessed | tf_op | source)
XLA Modules:
  0.0 76.5 jit_solution(3892223088761571646)
XLA Ops:
  0.6 0.0 copy-start
  0.6 1.1 %copy-done = f32[576,288]{0,1:T(8,128)S(1)} copy-done((f32[576,288]{0,1:T(8,128)S(1)}, f32[576,288]{0,1:T(8,128)}, u32[]{:S(2)}) %copy-start) | copy-done | bytes 663576
  1.7 0.0 copy-start.1
  1.7 0.9 %copy-done.1 = f32[18,1024]{1,0:T(8,128)S(1)} copy-done((f32[18,1024]{1,0:T(8,128)S(1)}, f32[18,1024]{1,0:T(8,128)}, u32[]{:S(2)}) %copy-start.1) | copy-done | bytes 73752
  2.6 0.0 copy-start.2
  2.6 0.7 copy-done.2
  3.4 69.8 %exchange.1 = (f32[192,192]{1,0:T(8,128)S(1)}, f32[4,216,128]{2,1,0:T(8,128)S(1)}, f32[2,8,32,128]{3,2,1,0:T(8,128)S(1)}, f32[2,4,8,24,128]{4,3,2,1,0:T(8,128)S(...) custom-call(f32[288,576]{1,0:T(8,128)S(1)} %bitcast.4, f32[18,192]{1,0:T(8,128)S(1)} %bitcast.5, f32[18,1024]{1,0:T(8,128)S(1)} %copy-done.1), custom_call_target="tpu_custom_call" | custom-call | tf_op jit(solution)/shard_map/exchange/pallas_call | solution.py:395
  73.1 0.0 copy-start.3
  73.1 0.7 copy-done.3
  73.8 2.7 %update.1 = (f32[288,576]{1,0:T(8,128)}, f32[18,1024]{1,0:T(8,128)}) custom-call(f32[192,192]{1,0:T(8,128)S(1)} %get-tuple-element.10.inv, f32[4,216,128]{2,1,0:T(8,128)S(1)} %get-tuple-element.11.pr, f32[2,8,32,128]{3,2,1,0:T(8,128)S(1)} %get-tuple-element.12.pc, f32[2,4,8,24,128]{4,3,2,1,0:T(8,128)S(1)} %get-tuple-element.13.pd, ...), custom_call_target="tpu_custom_call" | custom-call | tf_op jit(solution)/shard_map/update/pallas_call | solution.py:420
Async XLA Ops:
  0.6 1.1 %copy-start = (f32[576,288]{0,1:T(8,128)S(1)}, f32[576,288]{0,1:T(8,128)}, u32[]{:S(2)}) copy-start(f32[576,288]{0,1:T(8,128)} %param.4) | copy-start | bytes 1990660
  1.7 0.9 %copy-start.1 = (f32[18,1024]{1,0:T(8,128)S(1)}, f32[18,1024]{1,0:T(8,128)}, u32[]{:S(2)}) copy-start(f32[18,1024]{1,0:T(8,128)} %win.1) | copy-start | bytes 221188
  2.6 0.7 copy-start.2
  73.1 0.7 copy-start.3

commit v4 on v3

--- a/solution.py
+++ b/solution.py
@@ -59,27 +59,67 @@
     return m
 
 
+def product(a, b):
+    out = []
+    for row in a:
+        line = []
+        for j in range(len(b[0])):
+            t = [row[i] * b[i][j] for i in range(len(b))]
+            while len(t) > 1:
+                t = [t[i] + t[i + 1] for i in range(0, len(t), 2)]
+            line.append(t[0])
+        out.append(line)
+    return out
+
+
+def flipped(a):
+    return [list(r) for r in zip(*a)]
+
+
+def inverse_of_8(d):
+    four = range(4)
+    p = inverse_of_4([r[:4] for r in d[:4]])
+    q = [r[4:] for r in d[:4]]
+    w = product(p, q)
+    qw = product(flipped(q), w)
+    i4 = inverse_of_4([[d[4 + i][4 + j] - qw[i][j] for j in four] for i in four])
+    v = product(w, i4)
+    u = product(v, flipped(w))
+    m = [[None] * 8 for _ in range(8)]
+    for i in four:
+        for j in four:
+            m[4 + i][4 + j] = i4[i][j]
+            m[i][4 + j] = -v[i][j]
+            m[4 + j][i] = -v[i][j]
+            m[i][j] = p[i][j] + u[i][j]
+    return m
+
+
 def inverse_of_block(block):
     n = block.shape[0]
     lane = lax.broadcasted_iota(jnp.int32, (8, n), 1)
     sub = lax.broadcasted_iota(jnp.int32, (8, n), 0)
     tiles = [block[8 * t : 8 * t + 8, :] for t in range(n // 8)]
-    four = range(4)
-    for j in range(0, n, 4):
-        t0, s0 = j // 8, j % 8
-        cols = [[wide(t[:, j + a : j + a + 1], n) for a in four] for t in tiles]
-        rows = [wide(tiles[t0][s0 + a : s0 + a + 1, :], n) for a in four]
-        m = inverse_of_4([[wide(cols[t0][c][s0 + a : s0 + a + 1, :], n) for c in four] for a in four])
-        inside = (lane >= j) & (lane < j + 4)
-        rows = [jnp.where(inside, jnp.where(lane == j + a, 1.0, 0.0), rows[a]) for a in four]
-        g = [m[a][0] * rows[0] + m[a][1] * rows[1] + (m[a][2] * rows[2] + m[a][3] * rows[3]) for a in four]
+    eight = range(8)
+    for t0 in range(n // 8):
+        j = 8 * t0
+        cols = [[wide(t[:, j + a : j + a + 1], n) for a in eight] for t in tiles]
+        rows = [wide(tiles[t0][a : a + 1, :], n) for a in eight]
+        pivots = [[None] * 8 for _ in eight]
+        for a in eight:
+            for c in range(a, 8):
+                pivots[a][c] = pivots[c][a] = wide(cols[t0][c][a : a + 1, :], n)
+        m = inverse_of_8(pivots)
+        inside = (lane >= j) & (lane < j + 8)
+        rows = [jnp.where(inside, jnp.where(lane == j + a, 1.0, 0.0), rows[a]) for a in eight]
+        g = [r[0] for r in product(m, [[r] for r in rows])]
         for t in range(n // 8):
-            v = jnp.where(inside, 0.0, tiles[t])
-            for a in four:
-                v = v - cols[t][a] * g[a]
             if t == t0:
-                for a in four:
-                    v = jnp.where(sub == s0 + a, g[a], v)
+                v = g[0]
+                for a in range(1, 8):
+                    v = jnp.where(sub == a, g[a], v)
+            else:
+                v = jnp.where(inside, 0.0, tiles[t]) - product([cols[t]], [[r] for r in g])[0][0]
             tiles[t] = v
     return jnp.concatenate(tiles, axis=0)
 
@@ -235,6 +275,9 @@
     part = dot(xu[k], wg[...].reshape(NY * FP, CY), TN)
     for q in range(8):
         dr[q] = part[DR * q : DR * (q + 1), :]
+    for d in range(1, 8):
+        tx_, tk_ = other(x, d // 2, NX), other(k, d % 2, NK)
+        send(dr.at[2 * tx_ + tk_], drr.at[d], s_dx, at(xx=tx_, kk=tk_), d)
     got(s_x8, *range(1, 8))
     for i in range(8):
         unfold(x8c, (), F * i, x8[i])
@@ -254,31 +297,35 @@
     for d in range(1, 8):
         tx_, tk_ = other(x, d // 2, NX), other(k, d % 2, NK)
         send(ar.at[2 * tx_ + tk_], arr.at[d], s_ar, at(xx=tx_, kk=tk_), d)
-    for d in range(1, 8):
-        tx_, tk_ = other(x, d // 2, NX), other(k, d % 2, NK)
-        send(dr.at[2 * tx_ + tk_], drr.at[d], s_dx, at(xx=tx_, kk=tk_), d)
+    q_own = 2 * x + k
+    got(s_dx, *range(1, 8))
+    total = dr[q_own]
+    for d in range(1, 8):
+        total = total + drr[d]
+    d1[...] = total
+    for d in range(1, NZ):
+        send(d1, dzr.at[d], s_dz, at(zz=other(z, d, NZ)), d)
+
+    got(s_ar, *range(1, 8))
+    total = ar[q_own]
+    for d in range(1, 8):
+        total = total + arr[d]
+    a1[...] = total
+    for d in range(1, NZ):
+        send(a1, azr.at[d], s_az, at(zz=other(z, d, NZ)), d)
     for i in range(8):
         tp[i, 0:F, :] = ts[0, F * i : F * (i + 1), :]
         tp[i, F : F + 9, :] = ts[0, XF + 9 * i : XF + 9 * i + 9, :]
     for d in range(1, NZ):
         tz = other(z, d, NZ)
         send(tp.at[tz], tzr.at[d], s_tz, at(zz=tz), d)
-
-    got(s_ar, *range(1, 8))
-    q_own = 2 * x + k
-    total = ar[q_own]
-    for d in range(1, 8):
-        total = total + arr[d]
-    a1[...] = total
-    for d in range(1, NZ):
-        send(a1, azr.at[d], s_az, at(zz=other(z, d, NZ)), d)
-    got(s_dx, *range(1, 8))
-    total = dr[q_own]
-    for d in range(1, 8):
-        total = total + drr[d]
-    d1[...] = total
-    for d in range(1, NZ):
-        send(d1, dzr.at[d], s_dz, at(zz=other(z, d, NZ)), d)
+    got(s_dz, *range(1, NZ))
+    total = d1[...]
+    for d in range(1, NZ):
+        total = total + dzr[d]
+    dyr[y] = total
+    for d in range(1, NY):
+        send(dyr.at[y], dyr.at[y], s_dy, at(yy=other(y, d, NY)), d)
 
     got(s_az, *range(1, NZ))
     total = a1[...]
@@ -287,14 +334,6 @@
     ayr[y] = total
     for d in range(1, NY):
         send(ayr.at[y], ayr.at[y], s_ay, at(yy=other(y, d, NY)), d)
-
-    got(s_dz, *range(1, NZ))
-    total = d1[...]
-    for d in range(1, NZ):
-        total = total + dzr[d]
-    dyr[y] = total
-    for d in range(1, NY):
-        send(dyr.at[y], dyr.at[y], s_dy, at(yy=other(y, d, NY)), d)
     got(s_tz, *range(1, NZ))
     piece = tp[z]
     for d in range(1, NZ):
@@ -303,6 +342,11 @@
     for d in range(1, NZ):
         send(pz.at[z], pz.at[z], s_pz, at(zz=other(z, d, NZ)), d)
     send_far(pz.at[z], pc_out.at[gk, gy], s_pf, at(gy, gk, gx, gz))
+    got(s_dy, *range(1, NY))
+    pd_out[k, x] = dyr[...]
+    for d in range(1, NX):
+        send(pd_out.at[k, x], pd_out.at[k, x], s_d, at(xx=other(x, d, NX)), d)
+
 
     got(s_ay, *range(1, NY))
     total = ayr[0]
@@ -322,10 +366,8 @@
     got(s_pf)
     for d in range(1, NY):
         send(pc_out.at[k, y], pc_out.at[k, y], s_pc, at(yy=other(y, d, NY)), d)
-    got(s_dy, *range(1, NY))
-    pd_out[k, x] = dyr[...]
-    for d in range(1, NX):
-        send(pd_out.at[k, x], pd_out.at[k, x], s_d, at(xx=other(x, d, NX)), d)
+    got(s_d, *range(1, NX))
+    send(pd_out.at[k], pd_out.at[k], s_dk, at(kk=1 - k))
 
     got(s_s, *range(1, 8))
     h = 64
@@ -345,8 +387,6 @@
         if n == 0:
             got(s_pc, *range(1, 8))
             send(pc_out.at[k], pc_out.at[k], s_pck, at(kk=1 - k))
-            got(s_d, *range(1, NX))
-            send(pd_out.at[k], pd_out.at[k], s_dk, at(kk=1 - k))
     got(s_px, *range(1, NX))
     got(s_pck)
     got(s_dk)

time: 76.7 us -> 73.1 us (0.953)
  Pallas kernels: 72.4 us -> 68.2 us
    pallas_call x1, Pallas kernels: 69.8 us -> 65.5 us  [on_device(): pl.pallas_call(exchange_kernel, name='exchange', out_shape=tuple((jax.Sha...]
where the time goes in v4:
time: 73.1 us; the launch traced here: 72.2 us
  Pallas kernels  68.2 us (93%)
  local copies, waits for them, and re-layouts  3.41 us (5%)
    pallas_call x1, Pallas kernels, on_device(): pl.pallas_call(exchange_kernel, name='exchange', out_shape=tuple((jax.Sha...  65.5 us
    unnamed x8, local copies, waits for them, and re-layouts  3.41 us
    pallas_call x1, Pallas kernels, on_device(): pl.pallas_call(update_kernel, name='update', out_shape=(jax.ShapeDtypeStr...  2.65 us

profile of v4, /device:TPU:1, one launch (start us, length us, event | category | flops | bytes accessed | tf_op | source)
XLA Modules:
  0.0 72.2 jit_solution(3427617673575381580)
XLA Ops:
  0.6 0.0 copy-start
  0.6 1.1 %copy-done = f32[576,288]{0,1:T(8,128)S(1)} copy-done((f32[576,288]{0,1:T(8,128)S(1)}, f32[576,288]{0,1:T(8,128)}, u32[]{:S(2)}) %copy-start) | copy-done | bytes 663576
  1.7 0.0 copy-start.1
  1.7 0.9 %copy-done.1 = f32[18,1024]{1,0:T(8,128)S(1)} copy-done((f32[18,1024]{1,0:T(8,128)S(1)}, f32[18,1024]{1,0:T(8,128)}, u32[]{:S(2)}) %copy-start.1) | copy-done | bytes 73752
  2.6 0.0 copy-start.2
  2.6 0.7 %copy-done.2 = f32[192,18]{0,1:T(8,128)S(1)} copy-done((f32[192,18]{0,1:T(8,128)S(1)}, f32[192,18]{0,1:T(8,128)}, u32[]{:S(2)}) %copy-start.2) | copy-done | bytes 13848
  3.4 65.5 %exchange.1 = (f32[192,192]{1,0:T(8,128)S(1)}, f32[4,216,128]{2,1,0:T(8,128)S(1)}, f32[2,8,32,128]{3,2,1,0:T(8,128)S(1)}, f32[2,4,8,24,128]{4,3,2,1,0:T(8,128)S(...) custom-call(f32[288,576]{1,0:T(8,128)S(1)} %bitcast.4, f32[18,192]{1,0:T(8,128)S(1)} %bitcast.5, f32[18,1024]{1,0:T(8,128)S(1)} %copy-done.1), custom_call_target="tpu_custom_call" | custom-call | tf_op jit(solution)/shard_map/exchange/pallas_call | solution.py:435
  68.9 0.0 copy-start.3
  68.9 0.7 copy-done.3
  69.6 2.7 %update.1 = (f32[288,576]{1,0:T(8,128)}, f32[18,1024]{1,0:T(8,128)}) custom-call(f32[192,192]{1,0:T(8,128)S(1)} %get-tuple-element.10.inv, f32[4,216,128]{2,1,0:T(8,128)S(1)} %get-tuple-element.11.pr, f32[2,8,32,128]{3,2,1,0:T(8,128)S(1)} %get-tuple-element.12.pc, f32[2,4,8,24,128]{4,3,2,1,0:T(8,128)S(1)} %get-tuple-element.13.pd, ...), custom_call_target="tpu_custom_call" | custom-call | tf_op jit(solution)/shard_map/update/pallas_call | solution.py:460
Async XLA Ops:
  0.6 1.1 %copy-start = (f32[576,288]{0,1:T(8,128)S(1)}, f32[576,288]{0,1:T(8,128)}, u32[]{:S(2)}) copy-start(f32[576,288]{0,1:T(8,128)} %param.4) | copy-start | bytes 1990660
  1.7 0.9 %copy-start.1 = (f32[18,1024]{1,0:T(8,128)S(1)}, f32[18,1024]{1,0:T(8,128)}, u32[]{:S(2)}) copy-start(f32[18,1024]{1,0:T(8,128)} %win.1) | copy-start | bytes 221188
  2.6 0.7 %copy-start.2 = (f32[192,18]{0,1:T(8,128)S(1)}, f32[192,18]{0,1:T(8,128)}, u32[]{:S(2)}) copy-start(f32[192,18]{0,1:T(8,128)} %param.5) | copy-start | bytes 41476
  68.9 0.7 copy-start.3

commit v5 on v4

--- a/solution.py
+++ b/solution.py
@@ -153,7 +153,7 @@
 def exchange_kernel(
     cov, xin, win,
     inv_out, pr_out, pc_out, pd_out, rt, wt,
-    s_out, xt, rtp, rp, xpad, wst, xg, xu, x8, x8c, wg, ts, tr, tx, tp, tzr, pz, prc,
+    s_out, xt, rtp, rp, xpad, wst, xg, xu, x8, x8c, wg, th, ts, tr, tx, tp, tzr, pz, prc,
     ar, arr, a1, azr, ayr, asum, dr, drr, d1, dzr, dyr,
     lsem, ssem, s_xy, s_xk, s_xf, s_x8, s_w, s_t, s_ar, s_tz, s_az, s_ay, s_pz, s_pf, s_pc, s_pck, s_px, s_s, s_d, s_dk,
     s_dx, s_dz, s_dy,
@@ -228,7 +228,8 @@
     for q in range(16):
         r = 2 * (q % 8) + q // 8
         rtp[FP * q : FP * q + F, :] = rt[F * r : F * r + F, :]
-    rp[...] = rtp[...].T
+    for i in range(2):
+        rp[i] = rtp[NY * FP * i : NY * FP * (i + 1), :].T
 
     pl.semaphore_wait(barrier, 7 + 7 + 7 + 2 - 2 * is_own.astype(jnp.int32))
 
@@ -255,13 +256,14 @@
         send(wst.at[ty], wg.at[y], s_w, at(yy=ty), d)
     for j in range(NY):
         unfold(xu, (k,), FP * j, xg[k, j])
+    for d in (2, 1, 3, 0):
+        th[d] = dot(rp[k, pl.ds(pl.multiple_of(XF * other(x, d, NX), 16), XF), :], xu[k])
     got(s_xk)
     for j in range(NY):
         unfold(xu, (1 - k,), FP * j, xg[1 - k, j])
-    xct = xu[...].reshape(2 * NY * FP, B)
     for d in (2, 1, 3, 0):
         tx_ = other(x, d, NX)
-        t = dot(rp[pl.ds(pl.multiple_of(XF * tx_, 16), XF), :], xct)
+        t = th[d] + dot(rp[1 - k, pl.ds(pl.multiple_of(XF * tx_, 16), XF), :], xu[1 - k])
         ts[d, 0:XF, :] = t[:, 0:128]
         for i in range(8):
             ts[d, XF + 9 * i : XF + 9 * i + 9, 0:64] = t[F * i : F * i + 9, 128:192]
@@ -442,9 +444,9 @@
         in_specs=[pl.BlockSpec(memory_space=pltpu.HBM)] * 3,
         out_specs=(in_vmem,) * 6,
         scratch_shapes=[
-            vmem((8, SR, 128)), vmem((F, B)), vmem((16 * FP, RF)), vmem((RF, 16 * FP)),
+            vmem((8, SR, 128)), vmem((F, B)), vmem((16 * FP, RF)), vmem((2, RF, NY * FP)),
             vmem((PP, 128)), vmem((NY, FP, CY)), vmem((2, NY, PP, 128)), vmem((2, NY * FP, B)),
-            vmem((8, PP, 128)), vmem((XF, B)), vmem((NY, FP, CY)),
+            vmem((8, PP, 128)), vmem((XF, B)), vmem((NY, FP, CY)), vmem((NX, XF, B)),
             vmem((NX, XR, 128)), vmem((NX, XR, 128)), vmem((XF, B)), vmem((NZ, PP, 128)),
             vmem((NZ, PP, 128)), vmem((NZ, PP, 128)), vmem((XR, 128)),
             vmem((8, SR, 128)), vmem((8, SR, 128)), vmem((SR, 128)), vmem((NZ, SR, 128)), vmem((NY, SR, 128)),

time: 73.1 us -> 72.6 us (level)
  no operation moved by 1% of the time
where the time goes in v5:
time: 72.6 us; the launch traced here: 72.3 us
  Pallas kernels  68.2 us (94%)
  local copies, waits for them, and re-layouts  3.41 us (5%)
    pallas_call x1, Pallas kernels, on_device(): pl.pallas_call(exchange_kernel, name='exchange', out_shape=tuple((jax.Sha...  65.6 us
    unnamed x8, local copies, waits for them, and re-layouts  3.41 us
    pallas_call x1, Pallas kernels, on_device(): pl.pallas_call(update_kernel, name='update', out_shape=(jax.ShapeDtypeStr...  2.66 us

profile of v5, /device:TPU:1, one launch (start us, length us, event | category | flops | bytes accessed | tf_op | source)
XLA Modules:
  0.0 72.3 jit_solution(8285395355374797315)
XLA Ops:
  0.6 0.0 copy-start
  0.6 1.1 %copy-done = f32[576,288]{0,1:T(8,128)S(1)} copy-done((f32[576,288]{0,1:T(8,128)S(1)}, f32[576,288]{0,1:T(8,128)}, u32[]{:S(2)}) %copy-start) | copy-done | bytes 663576
  1.7 0.0 copy-start.1
  1.7 0.9 %copy-done.1 = f32[18,1024]{1,0:T(8,128)S(1)} copy-done((f32[18,1024]{1,0:T(8,128)S(1)}, f32[18,1024]{1,0:T(8,128)}, u32[]{:S(2)}) %copy-start.1) | copy-done | bytes 73752
  2.6 0.0 copy-start.2
  2.6 0.7 %copy-done.2 = f32[192,18]{0,1:T(8,128)S(1)} copy-done((f32[192,18]{0,1:T(8,128)S(1)}, f32[192,18]{0,1:T(8,128)}, u32[]{:S(2)}) %copy-start.2) | copy-done | bytes 13848
  3.4 65.6 %exchange.1 = (f32[192,192]{1,0:T(8,128)S(1)}, f32[4,216,128]{2,1,0:T(8,128)S(1)}, f32[2,8,32,128]{3,2,1,0:T(8,128)S(1)}, f32[2,4,8,24,128]{4,3,2,1,0:T(8,128)S(...) custom-call(f32[288,576]{1,0:T(8,128)S(1)} %bitcast.4, f32[18,192]{1,0:T(8,128)S(1)} %bitcast.5, f32[18,1024]{1,0:T(8,128)S(1)} %copy-done.1), custom_call_target="tpu_custom_call" | custom-call | tf_op jit(solution)/shard_map/exchange/pallas_call | solution.py:437
  69.0 0.0 copy-start.3
  69.0 0.7 copy-done.3
  69.6 2.7 %update.1 = (f32[288,576]{1,0:T(8,128)}, f32[18,1024]{1,0:T(8,128)}) custom-call(f32[192,192]{1,0:T(8,128)S(1)} %get-tuple-element.10.inv, f32[4,216,128]{2,1,0:T(8,128)S(1)} %get-tuple-element.11.pr, f32[2,8,32,128]{3,2,1,0:T(8,128)S(1)} %get-tuple-element.12.pc, f32[2,4,8,24,128]{4,3,2,1,0:T(8,128)S(1)} %get-tuple-element.13.pd, ...), custom_call_target="tpu_custom_call" | custom-call | tf_op jit(solution)/shard_map/update/pallas_call | solution.py:462
Async XLA Ops:
  0.6 1.1 %copy-start = (f32[576,288]{0,1:T(8,128)S(1)}, f32[576,288]{0,1:T(8,128)}, u32[]{:S(2)}) copy-start(f32[576,288]{0,1:T(8,128)} %param.4) | copy-start | bytes 1990660
  1.7 0.9 %copy-start.1 = (f32[18,1024]{1,0:T(8,128)S(1)}, f32[18,1024]{1,0:T(8,128)}, u32[]{:S(2)}) copy-start(f32[18,1024]{1,0:T(8,128)} %win.1) | copy-start | bytes 221188
  2.6 0.7 %copy-start.2 = (f32[192,18]{0,1:T(8,128)S(1)}, f32[192,18]{0,1:T(8,128)}, u32[]{:S(2)}) copy-start(f32[192,18]{0,1:T(8,128)} %param.5) | copy-start | bytes 41476
  69.0 0.7 copy-start.3
